TPU v7x, 512 devices: a whole 4x4x16 slice. The times are simulated.
512 devices in a mesh: cp: 64 (over z, x), tp: 8 (over y, core).
Axes of the slice: x: 4, y: 4, z: 16, core: 2. Of those that a mesh axis runs over, the one named last changes fastest.
Arguments:
- queries: bfloat16 [32, 512, 8192], P(None, 'cp', 'tp'), may hold values from -6 to 6
- key_row_matrix: bfloat16 [32, 512, 1024], P(None, 'cp', 'tp'), may hold values from -6 to 6
- value_row_matrix: bfloat16 [32, 512, 1024], P(None, 'cp', 'tp'), may hold values from -6 to 6
- residual: bfloat16 [32, 512, 4096], P(None, 'cp', 'tp'), may hold values from -6 to 6
- out_weight: bfloat16 [64, 128, 4096], P('tp', 'cp'), may hold values from -0.09375 to 0.09375
- doc_bounds: int32 [129], replicated, may hold values from 0 to 16384, as said below
- owner_plan: int32 [128], replicated, may hold values from 0 to 63, as said below
Outputs:
- mixed: bfloat16 [32, 512, 4096], P(None, 'cp', 'tp')
- stats: float32 [64, 64, 512], P('cp', 'tp')
Inputs may be any that keep to these rules, and one draw needn't show every extreme that they name: `doc_bounds`: increasing from 0 to 16384; every document length is a multiple of 8. `owner_plan`: each owner holds exactly two documents, and they are consecutive; the documents of one owner cover at most 64 blocks of 8 positions, and those of some owner exactly 64.
All inputs are finite; a program needn't handle non-finite values.
Results may differ from a plain program's by a relative error of at most 0.0034.
Values may be sent and summed in bfloat16 or wider, within the bound.
No kernel may reach another device: no remote copies, remote signals or barrier semaphores. Data moves between devices by JAX's collectives and lax.ppermute only.
A program may use at most 64 MiB of HBM per device.

v0:
```python
import math

import jax
import jax.numpy as jnp
from jax import lax
from jax.sharding import PartitionSpec as P

HEAD_SIZE = 128


MASKED = -1e30


def doc_lookup(doc_bounds, positions):
    return jnp.sum((doc_bounds[None, 1:] <= positions[:, None]).astype(jnp.int32), axis=1)


def owner_span(doc_bounds, owner_plan, owner, tokens, block_rows):
    mine = owner_plan == owner
    first_block = jnp.min(jnp.where(mine, doc_bounds[:-1], tokens)) // block_rows
    end_block = jnp.max(jnp.where(mine, doc_bounds[1:], 0)) // block_rows
    return (first_block, end_block)


def slot_positions(first_block, end_block, slot_count, block_rows):
    slot_ids = jnp.arange(slot_count, dtype=jnp.int32)
    block_ids = first_block + jnp.mod(slot_ids - first_block, slot_count)
    row_offsets = jnp.arange(block_rows, dtype=jnp.int32)
    positions = (block_ids[:, None] * block_rows + row_offsets[None, :]).reshape(-1)
    is_live = jnp.repeat(block_ids < end_block, block_rows)
    return (positions, is_live)


def attend_block(
    query_part,
    key_part,
    value_part,
    query_pos,
    query_doc,
    query_live,
    key_pos,
    key_doc,
    key_live,
    group,
):
    scale = 1.0 / math.sqrt(HEAD_SIZE)
    allowed = (
        query_live[:, None]
        & key_live[None, :]
        & (query_doc[:, None] == key_doc[None, :])
        & (key_pos[None, :] <= query_pos[:, None])
    )
    allowed = allowed | (key_pos[None, :] == query_pos[:, None])
    head_ids = jnp.arange(query_part.shape[1], dtype=jnp.int32)

    def one_head(head):
        query_head = lax.dynamic_index_in_dim(query_part, head, 1, keepdims=False)
        key_head = lax.dynamic_index_in_dim(key_part, head // group, 1, keepdims=False)
        value_head = lax.dynamic_index_in_dim(value_part, head // group, 1, keepdims=False)
        scores = (
            jnp.einsum("qd,pd->qp", query_head, key_head, preferred_element_type=jnp.float32)
            * scale
        )
        scores = jnp.where(allowed, scores, MASKED)
        row_max = jnp.max(scores, axis=1, keepdims=True)
        expo = jnp.where(allowed, jnp.exp(scores - row_max), 0.0)
        total = jnp.sum(expo, axis=1, keepdims=True)
        weighted = (
            jnp.dot(expo.astype(jnp.bfloat16), value_head, preferred_element_type=jnp.float32)
            / total
        )
        return (weighted.astype(jnp.bfloat16), row_max[:, 0] + jnp.log(total[:, 0]))

    outputs, log_totals = lax.map(one_head, head_ids)
    log_totals = jnp.where(query_live[None, :], log_totals, 0.0)
    return (jnp.transpose(outputs, (1, 0, 2)), log_totals)


def local(queries, key_row_matrix, value_row_matrix, residual, out_weight, doc_bounds, owner_plan):
    cp_count = lax.axis_size("cp")
    self_index = lax.axis_index("cp")
    block_count, block_rows, query_width = queries.shape
    heads_here = query_width // HEAD_SIZE
    group = heads_here // (key_row_matrix.shape[2] // HEAD_SIZE)
    own_rows = cp_count * block_rows
    tokens = block_count * own_rows
    home_blocks = jnp.arange(block_count, dtype=jnp.int32) * cp_count + self_index
    home_docs = doc_lookup(doc_bounds, home_blocks * block_rows)
    doc_ids = jnp.arange(owner_plan.shape[0], dtype=jnp.int32)
    home_owner = jnp.sum(
        jnp.where(home_docs[:, None] == doc_ids[None, :], owner_plan[None, :], 0), axis=1
    )
    owner_ids = jnp.arange(cp_count, dtype=jnp.int32)
    matched = home_owner[None, :] == owner_ids[:, None]
    pick_block = jnp.sum(
        jnp.where(matched, jnp.arange(block_count, dtype=jnp.int32)[None, :], 0), axis=1
    )
    present = jnp.any(matched, axis=1)

    def pack_rows(source):
        taken_rows = jnp.take(source, pick_block, axis=0)
        return jnp.where(present[:, None, None], taken_rows, jnp.zeros((), source.dtype))

    got_query, got_key, got_value = (
        lax.all_to_all(pack_rows(queries), "cp", split_axis=0, concat_axis=0, tiled=True),
        lax.all_to_all(pack_rows(key_row_matrix), "cp", split_axis=0, concat_axis=0, tiled=True),
        lax.all_to_all(pack_rows(value_row_matrix), "cp", split_axis=0, concat_axis=0, tiled=True),
    )
    first_block, end_block = owner_span(doc_bounds, owner_plan, self_index, tokens, block_rows)
    positions, is_live = slot_positions(first_block, end_block, cp_count, block_rows)
    slot_docs = doc_lookup(doc_bounds, positions)
    query_all = got_query.reshape(own_rows, heads_here, HEAD_SIZE)
    key_all = got_key.reshape(own_rows, -1, HEAD_SIZE)
    value_all = got_value.reshape(own_rows, -1, HEAD_SIZE)
    attended, log_totals = attend_block(
        query_all,
        key_all,
        value_all,
        positions,
        slot_docs,
        is_live,
        positions,
        slot_docs,
        is_live,
        group,
    )
    returned = lax.all_to_all(
        attended.reshape(cp_count, block_rows, query_width),
        "cp",
        split_axis=0,
        concat_axis=0,
        tiled=True,
    )
    home_rows = jnp.take(returned, home_owner, axis=0).reshape(
        block_count * block_rows, heads_here, HEAD_SIZE
    )
    partial_sum = jnp.einsum(
        "thd,hdo->to",
        home_rows,
        lax.all_gather(out_weight, "cp", axis=1, tiled=True),
        preferred_element_type=jnp.float32,
    )
    summed = lax.psum_scatter(partial_sum, "tp", scatter_dimension=1, tiled=True)
    mixed = (residual.reshape(summed.shape).astype(jnp.float32) + summed).astype(jnp.bfloat16)
    return (mixed.reshape(residual.shape), log_totals.reshape(1, heads_here, own_rows))


def solution(mesh):
    placed = (
        P(None, "cp", "tp"),
        P(None, "cp", "tp"),
        P(None, "cp", "tp"),
        P(None, "cp", "tp"),
        P("tp", "cp", None),
        P(),
        P(),
    )
    return jax.shard_map(
        local,
        mesh=mesh,
        in_specs=placed,
        out_specs=(P(None, "cp", "tp"), P("cp", "tp", None)),
        check_vma=False,
    )
```

profile of v0, /device:TPU:4, one launch (start us, length us, event | category | flops | bytes accessed | tf_op | source)
XLA Modules:
  0.0 324.3 jit_solution(8692656634397259029)
XLA Ops:
  7.2 1.6 fusion.20
  8.9 0.8 select_reduce_fusion.1
  10.0 1.5 gather_fusion.3
  11.5 1.5 gather_fusion.2
  12.9 0.9 select_select_fusion.1
  13.8 18.6 %all-to-all-start.2 = ((bf16[64,8,128]{2,1,0:T(8,128)(2,1)}), bf16[64,8,128]{2,1,0:T(8,128)(2,1)S(1)}, u32[]{:S(2)}, u32[]{:S(2)}) async-start(bf16[64,8,128]{2,1,0:T(8,128)(2,1)} %get-tuple-element.128), calls=%async_computation.2 | async-start | bytes 262144 | tf_op jit(solution)/shard_map/all_to_all | solution.py:107
  32.5 0.6 gather_fusion
  33.1 1.3 select_select_fusion
  34.4 13.9 %all-to-all-done.2 = bf16[64,8,128]{2,1,0:T(8,128)(2,1)S(1)} async-done(((bf16[64,8,128]{2,1,0:T(8,128)(2,1)}), bf16[64,8,128]{2,1,0:T(8,128)(2,1)S(1)}, u32[]{:S(2)}, u32[]{:S(2)}) %all-to-all-start.2) | async-done | bytes 131104 | tf_op jit(solution)/shard_map/all_to_all | solution.py:107
  48.3 6.4 %all-to-all-start = ((bf16[64,8,1024]{2,1,0:T(8,128)(2,1)}), bf16[64,8,1024]{2,1,0:T(8,128)(2,1)S(1)}, u32[]{:S(2)}, u32[]{:S(2)}) async-start(bf16[64,8,1024]{2,1,0:T(8,128)(2,1)} %select_select_fusion), calls=%async_computation | async-start | bytes 2097152 | tf_op jit(solution)/shard_map/all_to_all | solution.py:105
  54.7 1.6 copy.21
  61.7 51.0 %all-to-all-done = bf16[64,8,1024]{2,1,0:T(8,128)(2,1)S(1)} async-done(((bf16[64,8,1024]{2,1,0:T(8,128)(2,1)}), bf16[64,8,1024]{2,1,0:T(8,128)(2,1)S(1)}, u32[]{:S(2)}, u32[]{:S(2)}) %all-to-all-start) | async-done | bytes 1048608 | tf_op jit(solution)/shard_map/all_to_all | solution.py:105
  112.7 6.1 %all-to-all-start.1 = ((bf16[64,8,128]{2,1,0:T(8,128)(2,1)}), bf16[64,8,128]{2,1,0:T(8,128)(2,1)S(1)}, u32[]{:S(2)}, u32[]{:S(2)}) async-start(bf16[64,8,128]{2,1,0:T(8,128)(2,1)} %get-tuple-element.129), calls=%async_computation.1 | async-start | bytes 262144 | tf_op jit(solution)/shard_map/all_to_all | solution.py:106
  119.8 14.8 %all-to-all-done.1 = bf16[64,8,128]{2,1,0:T(8,128)(2,1)S(1)} async-done(((bf16[64,8,128]{2,1,0:T(8,128)(2,1)}), bf16[64,8,128]{2,1,0:T(8,128)(2,1)S(1)}, u32[]{:S(2)}, u32[]{:S(2)}) %all-to-all-start.1) | async-done | bytes 131104 | tf_op jit(solution)/shard_map/all_to_all | solution.py:106
  134.6 35.9 %while.14 = (s32[]{:T(128)}, bf16[8,512,128]{2,1,0:T(8,128)(2,1)S(1)}, f32[8,512]{1,0:T(8,128)S(1)}, s32[8]{0:T(128)S(1)}, bf16[512,8,128]{2,0,1:T(8,128)(2,1)S(...) while((s32[]{:T(128)}, ...), condition=%wide.region_10.12_spmd.clone.clone, body=%wide.region_7.11_spmd.clone.sunk.clone | while | flops 142212608 | bytes 3713703 | solution.py:74
  136.9 0.6 fusion.41
  137.5 0.6 fusion.42
  138.1 0.9 fusion.43
  141.4 0.6 fusion.41
  142.0 0.6 fusion.42
  142.6 0.9 fusion.43
  145.9 0.6 fusion.41
  146.5 0.6 fusion.42
  147.1 0.9 fusion.43
  150.3 0.6 fusion.41
  151.0 0.6 fusion.42
  151.6 0.9 fusion.43
  154.8 0.6 fusion.41
  155.4 0.6 fusion.42
  156.1 0.9 fusion.43
  159.3 0.6 fusion.41
  159.9 0.6 fusion.42
  160.5 0.9 fusion.43
  163.8 0.6 fusion.41
  164.4 0.6 fusion.42
  165.0 0.9 fusion.43
  168.3 0.6 fusion.41
  168.9 0.6 fusion.42
  169.5 0.9 fusion.43
  170.5 0.7 copy.20
  171.2 1.4 reshape.150
  172.5 6.6 %all-to-all-start.3 = ((bf16[64,8,1024]{2,1,0:T(8,128)(2,1)}), bf16[64,8,1024]{2,1,0:T(8,128)(2,1)S(1)}, u32[]{:S(2)}, u32[]{:S(2)}) async-start(bf16[64,8,1024]{2,1,0:T(8,128)(2,1)} %reshape.150), calls=%async_computation.3 | async-start | bytes 2097152 | tf_op jit(solution)/shard_map/all_to_all | solution.py:127
  179.5 64.8 %all-to-all-done.3 = bf16[64,8,1024]{2,1,0:T(8,128)(2,1)S(1)} async-done(((bf16[64,8,1024]{2,1,0:T(8,128)(2,1)}), bf16[64,8,1024]{2,1,0:T(8,128)(2,1)S(1)}, u32[]{:S(2)}, u32[]{:S(2)}) %all-to-all-start.3) | async-done | bytes 1048608 | tf_op jit(solution)/shard_map/all_to_all | solution.py:127
  246.0 20.0 %all-gather.2.cloned.1.call-done = bf16[8,128,4096]{2,0,1:T(8,128)(2,1)} async-done(((bf16[8,2,4096]{2,0,1:T(8,128)(2,1)}), bf16[8,128,4096]{2,0,1:T(8,128)(2,1)}) %all-gather.2.cloned.1.call-update) | async-done | bytes 8388624 | tf_op jit(solution)/shard_map/all_gather | solution.py:140
  265.9 7.8 %convolution_bitcast_fusion = f32[256,4096]{1,0:T(8,128)} fusion(bf16[256,8,128]{0,1,2:T(8,128)(2,1)S(1)} %copy.22, bf16[8,128,4096]{2,0,1:T(8,128)(2,1)} %all-gather.2.cloned.1.call-done), kind=kOutput, calls=%fused_computation.24 | convolution fusion | flops 2147483648 | bytes 13107200 | tf_op jit(solution)/shard_map/thd,hdo->to/dot_general | solution.py:137
  273.7 0.6 select_bitcast_fusion
  274.3 41.4 %reduce-scatter.2.cloned.1.call-done = f32[256,512]{1,0:T(8,128)} async-done(((f32[256,4096]{1,0:T(8,128)}), f32[256,512]{1,0:T(8,128)}) %reduce-scatter.2.cloned.1.call-update) | async-done | bytes 524304 | tf_op jit(solution)/shard_map/reduce_scatter | solution.py:143
  315.7 1.8 fusion.18
  (62 shorter events, 8.5 us)
Async XLA Ops:
  7.2 25.3 %copy-start = (bf16[32,8,1024]{2,1,0:T(8,128)(2,1)S(1)}, bf16[32,8,1024]{2,1,0:T(8,128)(2,1)}, u32[]{:S(2)}) copy-start(bf16[32,8,1024]{2,1,0:T(8,128)(2,1)} %param.11) | copy-start | bytes 1572868
  13.8 34.5 %all-to-all-start.2 = ((bf16[64,8,128]{2,1,0:T(8,128)(2,1)}), bf16[64,8,128]{2,1,0:T(8,128)(2,1)S(1)}, u32[]{:S(2)}, u32[]{:S(2)}) async-start(bf16[64,8,128]{2,1,0:T(8,128)(2,1)} %get-tuple-element.128), calls=%async_computation.2 | async-start | bytes 262144 | tf_op jit(solution)/shard_map/all_to_all | solution.py:107
  48.3 64.4 %all-to-all-start = ((bf16[64,8,1024]{2,1,0:T(8,128)(2,1)}), bf16[64,8,1024]{2,1,0:T(8,128)(2,1)S(1)}, u32[]{:S(2)}, u32[]{:S(2)}) async-start(bf16[64,8,1024]{2,1,0:T(8,128)(2,1)} %select_select_fusion), calls=%async_computation | async-start | bytes 2097152 | tf_op jit(solution)/shard_map/all_to_all | solution.py:105
  54.7 211.2 %all-gather.2.cloned.1.call-start = ((), (), s32[]{:S(2)}) async-start(), calls=%async_computation.5 | async-start | bytes 8519680 | tf_op jit(solution)/shard_map/all_gather | solution.py:140
  112.7 21.9 %all-to-all-start.1 = ((bf16[64,8,128]{2,1,0:T(8,128)(2,1)}), bf16[64,8,128]{2,1,0:T(8,128)(2,1)S(1)}, u32[]{:S(2)}, u32[]{:S(2)}) async-start(bf16[64,8,128]{2,1,0:T(8,128)(2,1)} %get-tuple-element.129), calls=%async_computation.1 | async-start | bytes 262144 | tf_op jit(solution)/shard_map/all_to_all | solution.py:106
  172.5 71.8 %all-to-all-start.3 = ((bf16[64,8,1024]{2,1,0:T(8,128)(2,1)}), bf16[64,8,1024]{2,1,0:T(8,128)(2,1)S(1)}, u32[]{:S(2)}, u32[]{:S(2)}) async-start(bf16[64,8,1024]{2,1,0:T(8,128)(2,1)} %reshape.150), calls=%async_computation.3 | async-start | bytes 2097152 | tf_op jit(solution)/shard_map/all_to_all | solution.py:127
  179.1 136.6 %reduce-scatter.2.cloned.1.call-start = ((), (), s32[]{:S(2)}) async-start(), calls=%async_computation.6 | async-start | bytes 4718592 | tf_op jit(solution)/shard_map/reduce_scatter | solution.py:143
  245.9 69.7 %copy-start.1 = (bf16[32,8,512]{2,1,0:T(8,128)(2,1)S(1)}, bf16[32,8,512]{2,1,0:T(8,128)(2,1)}, u32[]{:S(2)}) copy-start(bf16[32,8,512]{2,1,0:T(8,128)(2,1)} %param.14) | copy-start | bytes 786436
Sparse Core Ops, SparseCore 0:
  59.0 206.8 all-gather.1
  273.8 41.7 reduce-scatter.1
where the time goes:
time: 325 us; the launch traced here: 324 us
  waiting for transfers between devices  206 us (63%)
  starting transfers between devices  37.9 us (12%)
  matrix products  19.8 us (6%)
  between operations  19.6 us (6%)
  local copies, waits for them, and re-layouts  14.3 us (4%)
  loops' own time  14 us (4%)
  other arithmetic  13.1 us (4%)
    all_to_all x1, waiting for transfers between devices, local(): lax.all_to_all(attended.reshape(cp_count, block_rows, query_width), 'cp',...  64.8 us
    all_to_all x1, waiting for transfers between devices, local(): lax.all_to_all(pack_rows(queries), 'cp', split_axis=0, concat_axis=0, til...  51 us
    reduce_scatter x1, waiting for transfers between devices, local(): lax.psum_scatter(partial_sum, 'tp', scatter_dimension=1, tiled=True)  41.4 us
    all_gather x1, waiting for transfers between devices, local(): lax.all_gather(out_weight, 'cp', axis=1, tiled=True)  20 us
    all_to_all x1, starting transfers between devices, local(): lax.all_to_all(pack_rows(value_row_matrix), 'cp', split_axis=0, concat_ax...  18.6 us
    all_to_all x1, waiting for transfers between devices, local(): lax.all_to_all(pack_rows(key_row_matrix), 'cp', split_axis=0, concat_axis...  14.8 us
    another operation x1, loops' own time, attend_block(): outputs, log_totals = lax.map(one_head, head_ids)  14 us
    all_to_all x1, waiting for transfers between devices, local(): lax.all_to_all(pack_rows(value_row_matrix), 'cp', split_axis=0, concat_ax...  13.9 us
  transfers between devices with their start and end apart: 6, of which 6 were waited for; matrix products, arithmetic and copies ran while one was open for 10% of the time, Pallas kernels for 0%

commit v1 on v0

v1 whole, which is shorter than its diff:
```python
import math

import jax
import jax.numpy as jnp
from jax import lax
from jax.experimental import pallas as pl
from jax.experimental.pallas import tpu as pltpu
from jax.sharding import Mesh, PartitionSpec as P

HEAD_SIZE = 128
MASKED = -1e30
SCALE = 1.0 / math.sqrt(HEAD_SIZE)
LOG2E = math.log2(math.e)

AXES = ("zh", "zl", "x", "y", "c")
SIZES = (4, 4, 4, 4, 2)
CP = ("zh", "zl", "x")
TP = ("y", "c")
NEAR = ("zl", "x")

HEADS = 8
ROWS = 128


def attend_kernel(where_ref, bounds_ref, query_ref, far_ref, near_ref, out_ref, total_ref):
    zh, beta = where_ref[0], where_ref[1]
    row_iota = lax.broadcasted_iota(jnp.int32, (ROWS, ROWS), 0)
    lane_iota = lax.broadcasted_iota(jnp.int32, (ROWS, ROWS), 1)
    bounds = bounds_ref[...]
    for r in range(2):
        b = 2 * beta + r
        query_pos = 512 * b + 128 * zh + row_iota
        start = jnp.max(
            jnp.where(bounds <= query_pos, bounds, 0).astype(jnp.float32), axis=1, keepdims=True
        ).astype(jnp.int32)
        biases = []
        for zk in range(4):
            key_pos = 512 * (b - (zk >= zh).astype(jnp.int32)) + 128 * zk + lane_iota
            biases.append(jnp.where(key_pos >= start, 0.0, MASKED))
        key_pos = 512 * b + 128 * zh + lane_iota
        biases.append(jnp.where((key_pos >= start) & (key_pos <= query_pos), 0.0, MASKED))
        bias = jnp.concatenate(biases, axis=1)
        keys = jnp.concatenate([far_ref[zk, r, :, :HEAD_SIZE] for zk in range(4)] + [near_ref[r, :, :HEAD_SIZE]], axis=0)
        values = jnp.concatenate([far_ref[zk, r, :, HEAD_SIZE:] for zk in range(4)] + [near_ref[r, :, HEAD_SIZE:]], axis=0)
        columns = []
        for h in range(HEADS):
            lanes = slice(h * HEAD_SIZE, (h + 1) * HEAD_SIZE)
            scores = lax.dot_general(
                query_ref[r, :, lanes], keys, (((1,), (1,)), ((), ())),
                preferred_element_type=jnp.float32,
            ) + bias
            row_max = jnp.max(scores, axis=1, keepdims=True)
            expo = jnp.exp2((scores - row_max) * (SCALE * LOG2E))
            total = jnp.sum(expo, axis=1, keepdims=True)
            weighted = jnp.dot(expo.astype(jnp.bfloat16), values, preferred_element_type=jnp.float32)
            out_ref[r, :, lanes] = (weighted / total).astype(jnp.bfloat16)
            columns.append(row_max * SCALE + jnp.log(total))
        total_ref[r] = jnp.concatenate(columns, axis=1).T


def attend(where, bounds, query, far, near):
    vmem = pl.BlockSpec(memory_space=pltpu.VMEM)
    return pl.pallas_call(
        attend_kernel,
        out_shape=(
            jax.ShapeDtypeStruct((2, ROWS, HEADS * HEAD_SIZE), jnp.bfloat16),
            jax.ShapeDtypeStruct((2, HEADS, ROWS), jnp.float32),
        ),
        in_specs=[pl.BlockSpec(memory_space=pltpu.SMEM), vmem, vmem, vmem, vmem],
        out_specs=(vmem, vmem),
        compiler_params=pltpu.CompilerParams(vmem_limit_bytes=32 * 1024 * 1024),
        cost_estimate=pl.CostEstimate(
            flops=2 * 2 * 2 * 1024 * 640 * 128, bytes_accessed=2 * 1024 * 1024, transcendentals=2 * 1024 * 640
        ),
    )(where, bounds, query, far, near)


def swap(source, axes, split=0, concat=0):
    return lax.all_to_all(source, axes, split_axis=split, concat_axis=concat, tiled=True)


def local(queries, key_rows, value_rows, residual, out_weight, doc_bounds, owner_plan):
    bf16, f32, i32 = jnp.bfloat16, jnp.float32, jnp.int32
    zh, zl, x = (lax.axis_index(a).astype(i32) for a in CP)
    core = lax.axis_index("c")
    beta = 4 * zl + x

    weight = out_weight.reshape(8, 2, 4, 2, 4, 128).transpose(4, 1, 0, 3, 2, 5).reshape(8, 8, 1024)
    weight = swap(weight, "x")

    both = jnp.concatenate([key_rows, value_rows], axis=2)
    pairs = both.reshape(16, 2, 8, 256)
    before = jnp.concatenate([pairs[:1, 1:], pairs[:-1, 1:]], axis=0)
    near3 = swap(jnp.concatenate([before, pairs], axis=1), NEAR)
    near3 = near3.transpose(1, 0, 2, 3).reshape(3, ROWS, 256)
    targets = jnp.arange(4, dtype=i32)[:, None, None, None]
    far = swap(jnp.where(targets <= zh, near3[None, :2], near3[None, 1:]), "zh")

    query = swap(queries, NEAR, 0, 1)

    gathered = lax.all_gather(weight, ("zh", "zl"), axis=0, tiled=True)
    gathered = gathered.transpose(1, 0, 2).reshape(1024, 1024)

    attended, totals = attend(
        jnp.stack([zh, beta]), doc_bounds[:128].reshape(1, 128), query, far, near3[1:]
    )

    blocks = 64 * (2 * beta + jnp.arange(2, dtype=i32))[:, None] + 16 * zh + jnp.arange(16, dtype=i32)[None, :]
    docs = jnp.sum((doc_bounds[None, None, 1:] <= 8 * blocks[:, :, None]).astype(i32), axis=2)
    doc_ids = jnp.arange(128, dtype=i32)
    owners = jnp.sum(jnp.where(docs[:, :, None] == doc_ids, owner_plan, 0), axis=2)
    owners = jnp.repeat(owners, 8, axis=1)
    owner_ids = jnp.arange(64, dtype=i32)[:, None]
    packed = sum(
        jnp.where((owners[r][None, :] == owner_ids)[:, None, :], totals[r][None], 0.0) for r in range(2)
    )
    slots = swap(packed, CP).reshape(4, 16, 8, 128)
    stats = jnp.sum(slots, axis=1).transpose(1, 0, 2).reshape(1, 8, 512)

    attended = attended.reshape(1, 256, 1024)
    wide = swap(jnp.broadcast_to(attended, (4, 256, 1024)), "x").reshape(1024, 1024)
    halves = gathered.reshape(1024, 2, 512)
    theirs = jnp.dot(
        wide, lax.dynamic_index_in_dim(halves, 1 - core, 1, keepdims=False), preferred_element_type=f32
    ).astype(bf16)
    ours = jnp.dot(wide, lax.dynamic_index_in_dim(halves, core, 1, keepdims=False), preferred_element_type=f32)
    got = lax.ppermute(theirs, "c", [(0, 1), (1, 0)])
    pair = (ours + got.astype(f32)).astype(bf16)
    parts = swap(pair.reshape(1024, 4, 128).transpose(1, 0, 2), "y")
    summed = jnp.sum(parts.astype(f32), axis=0).astype(bf16)
    summed = summed.reshape(8, 16, 8, 128).transpose(1, 0, 2, 3)
    home = swap(summed, NEAR).reshape(4, 4, 8, 8, 128)
    home = home.transpose(0, 2, 3, 1, 4).reshape(32, 8, 512)
    mixed = (residual.astype(f32) + home.astype(f32)).astype(bf16)
    return mixed, stats


def solution(mesh):
    fine = Mesh(mesh.devices.reshape(SIZES), AXES)
    rows = P(None, CP, TP)
    return jax.shard_map(
        local,
        mesh=fine,
        in_specs=(rows, rows, rows, rows, P(TP, CP, None), P(), P()),
        out_specs=(rows, P(CP, TP, None)),
        check_vma=False,
    )
```

time: 325 us -> 223 us (0.69)
  the two profiles are of different devices: /device:TPU:4 before, /device:TPU:2 now
where the time goes in v1:
time: 223 us; the launch traced here: 222 us
  waiting for transfers between devices  113 us (51%)
  starting transfers between devices  54 us (24%)
  between operations  14.2 us (6%)
  blocking collectives  12.2 us (5%)
  local copies, waits for them, and re-layouts  10.9 us (5%)
  matrix products  8.12 us (4%)
  Pallas kernels  5.59 us (3%)
  other arithmetic  4.75 us (2%)
    all_to_all x7, waiting for transfers between devices, swap(): lax.all_to_all(source, axes, split_axis=split, concat_axis=concat, tiled=...  86.2 us
    all_to_all x7, starting transfers between devices, swap(): lax.all_to_all(source, axes, split_axis=split, concat_axis=concat, tiled=...  52.1 us
    all_gather x1, waiting for transfers between devices, local(): gathered = lax.all_gather(weight, ('zh', 'zl'), axis=0, tiled=True)  23.4 us
    all_to_all x1, blocking collectives, swap(): lax.all_to_all(source, axes, split_axis=split, concat_axis=concat, tiled=...  12.2 us
    pallas_call x1, Pallas kernels, attend(): pl.pallas_call(attend_kernel, out_shape=(jax.ShapeDtypeStruct((2, ROWS, H...  5.59 us
  transfers between devices with their start and end apart: 9, of which 8 were waited for; matrix products, arithmetic and copies ran while one was open for 6% of the time, Pallas kernels for 3%

profile of v1, /device:TPU:2, one launch (start us, length us, event | category | flops | bytes accessed | tf_op | source)
XLA Modules:
  0.0 222.5 jit_solution(14416013302880261192)
XLA Ops:
  7.2 1.0 reshape.141
  8.2 0.7 copy.59
  8.9 9.2 %all-to-all-start.4 = ((bf16[8,8,1024]{2,1,0:T(8,128)(2,1)}), bf16[8,8,1024]{2,1,0:T(8,128)(2,1)S(1)}, u32[]{:S(2)}, u32[]{:S(2)}) async-start(bf16[8,8,1024]{2,1,0:T(8,128)(2,1)} %bitcast.14), calls=%async_computation.4 | async-start | bytes 262144 | tf_op jit(solution)/shard_map/all_to_all | solution.py:79
  18.1 0.9 pad_maximum_fusion.1
  19.1 3.6 %all-to-all-done.4 = bf16[8,8,1024]{2,1,0:T(8,128)(2,1)S(1)} async-done(((bf16[8,8,1024]{2,1,0:T(8,128)(2,1)}), bf16[8,8,1024]{2,1,0:T(8,128)(2,1)S(1)}, u32[]{:S(2)}, u32[]{:S(2)}) %all-to-all-start.4) | async-done | bytes 131104 | tf_op jit(solution)/shard_map/all_to_all | solution.py:79
  22.7 12.2 %all_to_all.53 = bf16[16,3,8,256]{3,2,1,0:T(8,128)(2,1)S(1)} all-to-all(bf16[16,3,8,256]{3,2,1,0:T(8,128)(2,1)S(1)} %pad_maximum_fusion), channel_id=1, replica_groups=mesh['zh'=4,'zl'=4,'x'=4,'y'=4,'c'=2] {'zl','x'}, dimensions={0} | all-to-all | bytes 393216 | tf_op jit(solution)/shard_map/all_to_all | solution.py:79
  34.8 4.8 %all-to-all-start = ((bf16[32,8,1024]{2,1,0:T(8,128)(2,1)}), bf16[32,8,1024]{2,1,0:T(8,128)(2,1)S(1)}, u32[]{:S(2)}, u32[]{:S(2)}) async-start(bf16[32,8,1024]{2,1,0:T(8,128)(2,1)} %param.7), calls=%async_computation | async-start | bytes 1048576 | tf_op jit(solution)/shard_map/all_to_all | solution.py:79
  39.6 0.0 all-gather.2.cloned.1.call-start
  39.7 0.7 all-gather.2.cloned.1.call-update
  40.4 0.9 broadcast_select_fusion
  41.3 9.4 %all-to-all-done = bf16[32,8,1024]{2,1,0:T(8,128)(2,1)S(1)} async-done(((bf16[32,8,1024]{2,1,0:T(8,128)(2,1)}), bf16[32,8,1024]{2,1,0:T(8,128)(2,1)S(1)}, u32[]{:S(2)}, u32[]{:S(2)}) %all-to-all-start) | async-done | bytes 524320 | tf_op jit(solution)/shard_map/all_to_all | solution.py:79
  50.7 12.4 %all-to-all-start.2 = ((bf16[4,2,128,256]{3,2,1,0:T(8,128)(2,1)}), bf16[4,2,128,256]{3,2,1,0:T(8,128)(2,1)S(1)}, u32[]{:S(2)}, u32[]{:S(2)}) async-start(bf16[4,2,128,256]{3,2,1,0:T(8,128)(2,1)} %broadcast_select_fusion), calls=%async_computation.2 | async-start | bytes 1048576 | tf_op jit(solution)/shard_map/all_to_all | solution.py:79
  63.2 0.1 pad_add_fusion.where_ref
  63.2 0.0 copy-done.3
  63.2 0.1 fusion.9
  63.4 31.0 %all-to-all-done.2.far_ref = bf16[4,2,128,256]{3,2,1,0:T(8,128)(2,1)S(1)} async-done(((bf16[4,2,128,256]{3,2,1,0:T(8,128)(2,1)}), bf16[4,2,128,256]{3,2,1,0:T(8,128)(2,1)S(1)}, u32[]{:S(2)}, u32[]{:S(2)}) %all-to-all-start.2) | async-done | bytes 524320 | tf_op jit(solution)/shard_map/all_to_all | solution.py:79
  94.4 5.6 %shard_map.86 = (bf16[2,128,1024]{2,1,0:T(8,128)(2,1)S(1)}, f32[2,8,128]{2,1,0:T(8,128)S(1)}) custom-call(s32[2]{0:T(128)S(1)} %pad_add_fusion.where_ref, s32[1,128]{1,0:T(1,128)S(1)} %get-tuple-element.13.bounds_ref, bf16[2,128,1024]{2,1,0:T(8,128)(2,1)S(1)} %bitcast.63, bf16[4,2,128,256]{3,2,1,0:T(8,128)(2,1)S(1)} %all-to-all-done.2.far_ref, ...), custom_call_target="tpu_custom_call" | custom-call | flops 671088640 | bytes 2097152 | tf_op jit(solution)/shard_map/pallas_call | solution.py:63
  99.9 1.6 broadcast_in_dim.101
  101.6 6.2 %all-to-all-start.3 = ((bf16[4,256,1024]{2,1,0:T(8,128)(2,1)}), bf16[4,256,1024]{2,1,0:T(8,128)(2,1)}, u32[]{:S(2)}, u32[]{:S(2)}) async-start(bf16[4,256,1024]{2,1,0:T(8,128)(2,1)} %broadcast_in_dim.101), calls=%async_computation.3 | async-start | bytes 4194304 | tf_op jit(solution)/shard_map/all_to_all | solution.py:79
  107.8 23.4 %all-gather.2.cloned.1.call-done = bf16[128,8,1024]{2,1,0:T(8,128)(2,1)} async-done(((bf16[8,8,1024]{2,1,0:T(8,128)(2,1)}), bf16[128,8,1024]{2,1,0:T(8,128)(2,1)}) %all-gather.2.cloned.1.call-update) | async-done | bytes 2097168 | tf_op jit(solution)/shard_map/all_gather | solution.py:101
  131.2 3.7 %copy.60 = bf16[8,128,1024]{1,0,2:T(8,128)(2,1)S(1)} copy(bf16[8,128,1024]{2,0,1:T(8,128)(2,1)} %bitcast.64) | data formatting | bytes 4194304 | tf_op jit(solution)/shard_map/transpose | solution.py:102
  134.9 2.3 %reshape_reshape.3 = bf16[1024,2,512]{0,2,1:T(8,128)(2,1)} reshape(bf16[8,128,1024]{1,0,2:T(8,128)(2,1)S(1)} %copy.60) | data formatting | bytes 4194304 | tf_op jit(solution)/shard_map/reshape;reshape | solution.py:122
  137.2 0.0 all-to-all-done.3
  137.2 4.3 %convolution_convert_fusion = bf16[1024,512]{0,1:T(8,128)(2,1)} fusion(bf16[1024,1024]{1,0:T(8,128)(2,1)} %bitcast.11, bf16[1024,2,512]{0,2,1:T(8,128)(2,1)} %reshape_reshape.3, s32[]{:T(128)S(6)} %select_n.24), kind=kOutput, calls=%fused_computation.1 | convolution fusion | flops 1074266112 | bytes 4194308 | tf_op jit(solution)/shard_map/dot_general | solution.py:123
  141.5 1.9 collective-permute-start
  143.5 0.1 add_multiply_fusion
  143.5 0.2 convert_reduce_fusion
  143.7 0.2 select_reduce_fusion
  143.9 2.4 %collective-permute-done = bf16[1024,512]{0,1:T(8,128)(2,1)S(1)} collective-permute-done((bf16[1024,512]{0,1:T(8,128)(2,1)}, bf16[1024,512]{0,1:T(8,128)(2,1)S(1)}, u32[]{:S(2)}, u32[]{:S(2)}) %collective-permute-start) | collective-permute-done | bytes 1048608 | tf_op jit(solution)/shard_map/ppermute | solution.py:127
  146.3 3.8 %add_convert_fusion = bf16[1024,512]{0,1:T(8,128)(2,1)} fusion(bf16[1024,512]{0,1:T(8,128)(2,1)S(1)} %collective-permute-done, bf16[1024,1024]{1,0:T(8,128)(2,1)} %bitcast.11, bf16[1024,2,512]{0,2,1:T(8,128)(2,1)S(1)} %copy-done, s32[]{:T(128)S(6)} %select_n.23), kind=kOutput, calls=%fused_computation | convolution fusion | flops 1075314688 | bytes 5242884 | tf_op jit(solution)/shard_map/dot_general | solution.py:126
  150.1 4.5 %all-to-all-start.5 = ((bf16[4,1024,128]{1,2,0:T(8,128)(2,1)}), bf16[4,1024,128]{1,2,0:T(8,128)(2,1)S(1)}, u32[]{:S(2)}, u32[]{:S(2)}) async-start(bf16[4,1024,128]{1,2,0:T(8,128)(2,1)} %bitcast.19), calls=%async_computation.5 | async-start | bytes 2097152 | tf_op jit(solution)/shard_map/all_to_all | solution.py:79
  154.7 0.1 broadcast_in_dim.104
  154.7 0.1 eq.54
  154.8 0.1 broadcast_in_dim.109
  154.9 0.1 eq.58
  155.0 0.8 select_add_fusion
  155.8 14.3 %all-to-all-done.5 = bf16[4,1024,128]{1,2,0:T(8,128)(2,1)S(1)} async-done(((bf16[4,1024,128]{1,2,0:T(8,128)(2,1)}), bf16[4,1024,128]{1,2,0:T(8,128)(2,1)S(1)}, u32[]{:S(2)}, u32[]{:S(2)}) %all-to-all-start.5) | async-done | bytes 1048608 | tf_op jit(solution)/shard_map/all_to_all | solution.py:79
  170.0 10.3 %all-to-all-start.7 = ((f32[64,8,128]{2,1,0:T(8,128)}), f32[64,8,128]{2,1,0:T(8,128)S(1)}, u32[]{:S(2)}, u32[]{:S(2)}) async-start(f32[64,8,128]{2,1,0:T(8,128)} %select_add_fusion), calls=%async_computation.7 | async-start | bytes 524288 | tf_op jit(solution)/shard_map/all_to_all | solution.py:79
  180.3 0.2 reduce_sum.39
  180.5 0.0 copy-start.2
  180.5 0.2 copy.64
  180.7 0.8 copy.65
  181.5 20.0 %all-to-all-done.7 = f32[64,8,128]{2,1,0:T(8,128)S(1)} async-done(((f32[64,8,128]{2,1,0:T(8,128)}), f32[64,8,128]{2,1,0:T(8,128)S(1)}, u32[]{:S(2)}, u32[]{:S(2)}) %all-to-all-start.7) | async-done | bytes 262176 | tf_op jit(solution)/shard_map/all_to_all | solution.py:79
  201.5 4.6 %all-to-all-start.6 = ((bf16[16,8,8,128]{3,2,1,0:T(8,128)(2,1)}), bf16[16,8,8,128]{3,2,1,0:T(8,128)(2,1)S(1)}, u32[]{:S(2)}, u32[]{:S(2)}) async-start(bf16[16,8,8,128]{3,2,1,0:T(8,128)(2,1)} %copy.65), calls=%async_computation.6 | async-start | bytes 524288 | tf_op jit(solution)/shard_map/all_to_all | solution.py:79
  206.1 0.6 bitcast_reduce_fusion
  206.7 8.0 %all-to-all-done.6 = bf16[16,8,8,128]{3,2,1,0:T(8,128)(2,1)S(1)} async-done(((bf16[16,8,8,128]{3,2,1,0:T(8,128)(2,1)}), bf16[16,8,8,128]{3,2,1,0:T(8,128)(2,1)S(1)}, u32[]{:S(2)}, u32[]{:S(2)}) %all-to-all-start.6) | async-done | bytes 262176 | tf_op jit(solution)/shard_map/all_to_all | solution.py:79
  214.8 0.1 copy.66
  214.8 0.8 add_convert_fusion.1
  (20 shorter events, 0.2 us)
Async XLA Ops:
  8.9 13.7 %all-to-all-start.4 = ((bf16[8,8,1024]{2,1,0:T(8,128)(2,1)}), bf16[8,8,1024]{2,1,0:T(8,128)(2,1)S(1)}, u32[]{:S(2)}, u32[]{:S(2)}) async-start(bf16[8,8,1024]{2,1,0:T(8,128)(2,1)} %bitcast.14), calls=%async_computation.4 | async-start | bytes 262144 | tf_op jit(solution)/shard_map/all_to_all | solution.py:79
  22.6 17.0 %copy-start.1 = (bf16[8,8,1024]{2,1,0:T(8,128)(2,1)}, bf16[8,8,1024]{2,1,0:T(8,128)(2,1)S(1)}, u32[]{:S(2)}) copy-start(bf16[8,8,1024]{2,1,0:T(8,128)(2,1)S(1)} %all-to-all-done.4) | copy-start | bytes 393220
  22.7 40.6 %copy-start.3 = (s32[129]{0:T(256)S(1)}, s32[129]{0:T(256)}, u32[]{:S(2)}) copy-start(s32[129]{0:T(256)} %param.12) | copy-start | bytes 1552
  34.8 15.9 %all-to-all-start = ((bf16[32,8,1024]{2,1,0:T(8,128)(2,1)}), bf16[32,8,1024]{2,1,0:T(8,128)(2,1)S(1)}, u32[]{:S(2)}, u32[]{:S(2)}) async-start(bf16[32,8,1024]{2,1,0:T(8,128)(2,1)} %param.7), calls=%async_computation | async-start | bytes 1048576 | tf_op jit(solution)/shard_map/all_to_all | solution.py:79
  39.6 91.6 %all-gather.2.cloned.1.call-start = ((), (), s32[]{:S(2)}) async-start(), calls=%async_computation.8 | async-start | bytes 2228224 | tf_op jit(solution)/shard_map/all_gather | solution.py:101
  50.7 43.6 %all-to-all-start.2 = ((bf16[4,2,128,256]{3,2,1,0:T(8,128)(2,1)}), bf16[4,2,128,256]{3,2,1,0:T(8,128)(2,1)S(1)}, u32[]{:S(2)}, u32[]{:S(2)}) async-start(bf16[4,2,128,256]{3,2,1,0:T(8,128)(2,1)} %broadcast_select_fusion), calls=%async_computation.2 | async-start | bytes 1048576 | tf_op jit(solution)/shard_map/all_to_all | solution.py:79
  101.6 35.7 %all-to-all-start.3 = ((bf16[4,256,1024]{2,1,0:T(8,128)(2,1)}), bf16[4,256,1024]{2,1,0:T(8,128)(2,1)}, u32[]{:S(2)}, u32[]{:S(2)}) async-start(bf16[4,256,1024]{2,1,0:T(8,128)(2,1)} %broadcast_in_dim.101), calls=%async_computation.3 | async-start | bytes 4194304 | tf_op jit(solution)/shard_map/all_to_all | solution.py:79
  137.2 6.5 %copy-start.4 = (s32[128]{0:T(128)S(1)}, s32[128]{0:T(128)}, u32[]{:S(2)}) copy-start(s32[128]{0:T(128)} %param.13) | copy-start | bytes 1540
  137.2 9.0 %copy-start = (bf16[1024,2,512]{0,2,1:T(8,128)(2,1)S(1)}, bf16[1024,2,512]{0,2,1:T(8,128)(2,1)}, u32[]{:S(2)}) copy-start(bf16[1024,2,512]{0,2,1:T(8,128)(2,1)} %reshape_reshape.3) | copy-start | bytes 6291460
  141.5 4.8 %collective-permute-start = (bf16[1024,512]{0,1:T(8,128)(2,1)}, bf16[1024,512]{0,1:T(8,128)(2,1)S(1)}, u32[]{:S(2)}, u32[]{:S(2)}) collective-permute-start(bf16[1024,512]{0,1:T(8,128)(2,1)} %convolution_convert_fusion), channel_id=1, source_target_pairs={{0,1},{1,0},{2,3},{3,2},{4,5},{5,4},{6,7},{7,6},{8,9},{9,8},{10,11... | collective-permute-start | bytes 3145736 | tf_op jit(solution)/shard_map/ppermute | solution.py:127
  150.1 19.9 %all-to-all-start.5 = ((bf16[4,1024,128]{1,2,0:T(8,128)(2,1)}), bf16[4,1024,128]{1,2,0:T(8,128)(2,1)S(1)}, u32[]{:S(2)}, u32[]{:S(2)}) async-start(bf16[4,1024,128]{1,2,0:T(8,128)(2,1)} %bitcast.19), calls=%async_computation.5 | async-start | bytes 2097152 | tf_op jit(solution)/shard_map/all_to_all | solution.py:79
  170.0 31.4 %all-to-all-start.7 = ((f32[64,8,128]{2,1,0:T(8,128)}), f32[64,8,128]{2,1,0:T(8,128)S(1)}, u32[]{:S(2)}, u32[]{:S(2)}) async-start(f32[64,8,128]{2,1,0:T(8,128)} %select_add_fusion), calls=%async_computation.7 | async-start | bytes 524288 | tf_op jit(solution)/shard_map/all_to_all | solution.py:79
  180.5 34.3 %copy-start.2 = (bf16[32,8,512]{2,1,0:T(8,128)(2,1)S(1)}, bf16[32,8,512]{2,1,0:T(8,128)(2,1)}, u32[]{:S(2)}) copy-start(bf16[32,8,512]{2,1,0:T(8,128)(2,1)} %param.10) | copy-start | bytes 786436
  201.5 13.2 %all-to-all-start.6 = ((bf16[16,8,8,128]{3,2,1,0:T(8,128)(2,1)}), bf16[16,8,8,128]{3,2,1,0:T(8,128)(2,1)S(1)}, u32[]{:S(2)}, u32[]{:S(2)}) async-start(bf16[16,8,8,128]{3,2,1,0:T(8,128)(2,1)} %copy.65), calls=%async_computation.6 | async-start | bytes 524288 | tf_op jit(solution)/shard_map/all_to_all | solution.py:79
Sparse Core Ops, SparseCore 0:
  43.1 88.0 all-gather.1

commit v2 on v1

v2 whole, which is shorter than its diff:
```python
import math

import jax
import jax.numpy as jnp
from jax import lax
from jax.experimental import pallas as pl
from jax.experimental.pallas import tpu as pltpu
from jax.sharding import Mesh, PartitionSpec as P

HEAD_SIZE = 128
MASKED = -1e30
SCALE = 1.0 / math.sqrt(HEAD_SIZE)
LOG2E = math.log2(math.e)

AXES = ("za", "zb", "zl", "x", "y", "c")
SIZES = (2, 2, 4, 4, 4, 2)
CP = ("za", "zb", "zl", "x")
ZH = ("za", "zb")
Z = ("za", "zb", "zl")
TP = ("y", "c")
NEAR = ("zl", "x")

HEADS = 8
ROWS = 128


def attend_kernel(where_ref, bounds_ref, query_ref, far_ref, near_ref, out_ref, total_ref):
    zh, beta = where_ref[0], where_ref[1]
    row_iota = lax.broadcasted_iota(jnp.int32, (ROWS, ROWS), 0)
    lane_iota = lax.broadcasted_iota(jnp.int32, (ROWS, ROWS), 1)
    bounds = bounds_ref[...]
    for r in range(2):
        b = 2 * beta + r
        query_pos = 512 * b + 128 * zh + row_iota
        start = jnp.max(
            jnp.where(bounds <= query_pos, bounds, 0).astype(jnp.float32), axis=1, keepdims=True
        ).astype(jnp.int32)
        biases = []
        for step in range(4):
            zk = lax.rem(zh - step + 4, 4)
            key_pos = 512 * (b - (zk >= zh).astype(jnp.int32)) + 128 * zk + lane_iota
            biases.append(jnp.where(key_pos >= start, 0.0, MASKED))
        key_pos = 512 * b + 128 * zh + lane_iota
        biases.append(jnp.where((key_pos >= start) & (key_pos <= query_pos), 0.0, MASKED))
        bias = jnp.concatenate(biases, axis=1)
        keys = jnp.concatenate([far_ref[zk, r, :, :HEAD_SIZE] for zk in range(4)] + [near_ref[r, :, :HEAD_SIZE]], axis=0)
        values = jnp.concatenate([far_ref[zk, r, :, HEAD_SIZE:] for zk in range(4)] + [near_ref[r, :, HEAD_SIZE:]], axis=0)
        columns = []
        for h in range(HEADS):
            lanes = slice(h * HEAD_SIZE, (h + 1) * HEAD_SIZE)
            scores = lax.dot_general(
                query_ref[r, :, lanes], keys, (((1,), (1,)), ((), ())),
                preferred_element_type=jnp.float32,
            ) + bias
            row_max = jnp.max(scores, axis=1, keepdims=True)
            expo = jnp.exp2((scores - row_max) * (SCALE * LOG2E))
            total = jnp.sum(expo, axis=1, keepdims=True)
            weighted = jnp.dot(expo.astype(jnp.bfloat16), values, preferred_element_type=jnp.float32)
            rows = (weighted / total).astype(jnp.bfloat16)
            for copy in range(4):
                out_ref[copy, r, :, lanes] = rows
            columns.append(row_max * SCALE + jnp.log(total))
        total_ref[r] = jnp.concatenate(columns, axis=1).T


def attend(where, bounds, query, far, near):
    vmem = pl.BlockSpec(memory_space=pltpu.VMEM)
    return pl.pallas_call(
        attend_kernel,
        out_shape=(
            jax.ShapeDtypeStruct((4, 2, ROWS, HEADS * HEAD_SIZE), jnp.bfloat16),
            jax.ShapeDtypeStruct((2, HEADS, ROWS), jnp.float32),
        ),
        in_specs=[pl.BlockSpec(memory_space=pltpu.SMEM), vmem, vmem, vmem, vmem],
        out_specs=(vmem, vmem),
        compiler_params=pltpu.CompilerParams(vmem_limit_bytes=32 * 1024 * 1024),
        cost_estimate=pl.CostEstimate(
            flops=2 * 2 * 2 * 1024 * 640 * 128, bytes_accessed=2 * 1024 * 1024, transcendentals=2 * 1024 * 640
        ),
    )(where, bounds, query, far, near)


def project_kernel(rows_ref, weight_ref, out_ref):
    for part in range(4):
        rows = slice(part * 256, (part + 1) * 256)
        product = jnp.dot(rows_ref[rows], weight_ref[...], preferred_element_type=jnp.float32)
        for y in range(4):
            out_ref[y, rows] = product[:, y * 128 : (y + 1) * 128].astype(out_ref.dtype)


def project(rows, weight, half, dtype):
    vmem = pl.BlockSpec(memory_space=pltpu.VMEM)
    return pl.pallas_call(
        project_kernel,
        grid=(1,),
        out_shape=jax.ShapeDtypeStruct((4, 1024, 128), dtype),
        in_specs=[vmem, pl.BlockSpec((1024, 512), lambda i: (0, half))],
        out_specs=vmem,
        compiler_params=pltpu.CompilerParams(vmem_limit_bytes=32 * 1024 * 1024),
        cost_estimate=pl.CostEstimate(
            flops=2 * 1024 * 1024 * 512, bytes_accessed=4 * 1024 * 1024, transcendentals=0
        ),
    )(rows, weight)


def swap(source, axes, split=0, concat=0):
    return lax.all_to_all(source, axes, split_axis=split, concat_axis=concat, tiled=True)


def shift(source, axes, size, step):
    return lax.ppermute(source, axes, [(i, (i + step) % size) for i in range(size)])


def local(queries, key_rows, value_rows, residual, out_weight, doc_bounds, owner_plan):
    bf16, f32, i32 = jnp.bfloat16, jnp.float32, jnp.int32
    zh, zl, x = lax.axis_index(ZH), lax.axis_index("zl"), lax.axis_index("x")
    core = lax.axis_index("c")
    beta = 4 * zl + x

    weight = out_weight.reshape(8, 2, 4, 2, 4, 128)
    weight = jnp.where(core == 0, weight, jnp.flip(weight, 3)).transpose(4, 0, 1, 3, 2, 5).reshape(4, 8, 2, 1024)
    weight = swap(weight, "x").transpose(1, 0, 2, 3).reshape(8, 8, 1024)
    gathered = lax.all_gather(weight, Z, axis=0, tiled=False)
    gathered = gathered.transpose(1, 0, 2, 3).reshape(1024, 1024)

    both = jnp.concatenate([key_rows, value_rows], axis=2)
    pairs = both.reshape(16, 2, 8, 256)
    before = jnp.concatenate([pairs[:1, 1:], pairs[:-1, 1:]], axis=0)
    near3, weight = lax.optimization_barrier((jnp.concatenate([before, pairs], axis=1), weight))
    near3 = swap(near3, NEAR)
    near3 = near3.transpose(1, 0, 2, 3).reshape(3, ROWS, 256)

    far = [near3[:2]]
    for step in (1, 2, 3):
        rows = jnp.where(zh + step >= 4, near3[:2], near3[1:])
        far.append(shift(rows, ZH, 4, step))
    far = jnp.stack(far)

    queries, near3 = lax.optimization_barrier((queries, near3))
    query = swap(queries, NEAR, 0, 1)

    attended, totals = attend(
        jnp.stack([zh, beta]), doc_bounds[:128].reshape(1, 128), query, far, near3[1:]
    )

    totals = totals.astype(bf16)
    lanes = [totals] + [shift(totals, ZH, 4, step) for step in (1, 2, 3)]
    groups = [(zh - step) % 4 for step in range(4)]
    blocks = 64 * (2 * beta + jnp.arange(2, dtype=i32))[:, None, None] + jnp.arange(16, dtype=i32)
    blocks = blocks + 16 * jnp.stack(groups)[None, :, None]
    docs = jnp.sum((doc_bounds[1:] <= 8 * blocks[..., None]).astype(i32), axis=-1)
    owners = jnp.sum(jnp.where(docs[..., None] == jnp.arange(128, dtype=i32), owner_plan, 0), axis=-1)
    owners = jnp.repeat(owners, 8, axis=2) - 16 * zh
    receivers = jnp.arange(16, dtype=i32)[:, None, None, None]
    lanes = jnp.stack(lanes)
    packed = jnp.zeros((), bf16)
    for r in range(2):
        packed = packed + jnp.where(owners[r][None, :, None, :] == receivers, lanes[None, :, r], jnp.zeros((), bf16))

    wide = swap(attended.reshape(4, 256, 1024), "x").reshape(1024, 1024)
    wide, packed = lax.optimization_barrier((wide, packed))
    theirs = project(wide, gathered, 1, bf16)
    got = lax.ppermute(theirs, "c", [(0, 1), (1, 0)])
    ours = project(wide, gathered, 0, f32)
    ours, got = lax.optimization_barrier((ours, got))
    parts = swap((ours + got.astype(f32)).astype(bf16), "y")
    summed = jnp.sum(parts.astype(f32), axis=0).astype(bf16)
    summed = summed.reshape(8, 16, 8, 128).transpose(1, 0, 2, 3)
    home = swap(jnp.concatenate([summed, packed], axis=1), NEAR)
    stats = jnp.sum(home[:, 8:].astype(f32), axis=0)
    stats = jnp.concatenate([lax.dynamic_index_in_dim(stats, (zh - k) % 4, 0, keepdims=False) for k in range(4)], axis=1)
    stats = stats.reshape(1, 8, 512)
    home = home[:, :8].reshape(4, 4, 8, 8, 128).transpose(0, 2, 3, 1, 4).reshape(32, 8, 512)
    mixed = (residual.astype(f32) + home.astype(f32)).astype(bf16)
    return mixed, stats


def solution(mesh):
    fine = Mesh(mesh.devices.reshape(SIZES), AXES)
    rows = P(None, CP, TP)
    return jax.shard_map(
        local,
        mesh=fine,
        in_specs=(rows, rows, rows, rows, P(TP, CP, None), P(), P()),
        out_specs=(rows, P(CP, TP, None)),
        check_vma=False,
    )
```

time: 223 us -> 176 us (0.79)
  the two profiles are of different devices: /device:TPU:2 before, /device:TPU:8 now
where the time goes in v2:
time: 176 us; the launch traced here: 175 us
  starting transfers between devices  68.7 us (39%)
  waiting for transfers between devices  53.1 us (30%)
  blocking collectives  18.9 us (11%)
  between operations  14.5 us (8%)
  Pallas kernels  8.28 us (5%)
  local copies, waits for them, and re-layouts  6.88 us (4%)
  other arithmetic  4.73 us (3%)
    ppermute x6, starting transfers between devices, shift(): lax.ppermute(source, axes, [(i, (i + step) % size) for i in range(size)])  40.5 us
    all_to_all x5, starting transfers between devices, swap(): lax.all_to_all(source, axes, split_axis=split, concat_axis=concat, tiled=...  26.2 us
    all_to_all x5, waiting for transfers between devices, swap(): lax.all_to_all(source, axes, split_axis=split, concat_axis=concat, tiled=...  25 us
    ppermute x6, waiting for transfers between devices, shift(): lax.ppermute(source, axes, [(i, (i + step) % size) for i in range(size)])  23.8 us
    all_to_all x1, blocking collectives, swap(): lax.all_to_all(source, axes, split_axis=split, concat_axis=concat, tiled=...  18.9 us
    pallas_call x1, Pallas kernels, attend(): pl.pallas_call(attend_kernel, out_shape=(jax.ShapeDtypeStruct((4, 2, ROWS...  5.79 us
  transfers between devices with their start and end apart: 13, of which 8 were waited for; matrix products, arithmetic and copies ran while one was open for 2% of the time, Pallas kernels for 4%

profile of v2, /device:TPU:8, one launch (start us, length us, event | category | flops | bytes accessed | tf_op | source)
XLA Modules:
  0.0 175.0 jit_solution(10175184884442083240)
XLA Ops:
  7.2 1.0 reshape.149
  8.3 0.1 fusion
  8.3 0.7 reshape.150
  9.1 4.3 %all-to-all-start.3 = ((bf16[4,8,2,1024]{3,1,2,0:T(8,128)(2,1)}), bf16[4,8,2,1024]{3,1,2,0:T(8,128)(2,1)S(1)}, u32[]{:S(2)}, u32[]{:S(2)}) async-start(bf16[4,8,2,1024]{3,1,2,0:T(8,128)(2,1)} %reshape.150), calls=%async_computation.3 | async-start | bytes 262144 | tf_op jit(solution)/shard_map/all_to_all | solution.py:107
  13.4 0.9 pad_maximum_fusion.3
  14.3 0.7 pad_maximum_fusion.2
  15.0 4.4 %all-to-all-done.3 = bf16[4,8,2,1024]{3,1,2,0:T(8,128)(2,1)S(1)} async-done(((bf16[4,8,2,1024]{3,1,2,0:T(8,128)(2,1)}), bf16[4,8,2,1024]{3,1,2,0:T(8,128)(2,1)S(1)}, u32[]{:S(2)}, u32[]{:S(2)}) %all-to-all-start.3) | async-done | bytes 131104 | tf_op jit(solution)/shard_map/all_to_all | solution.py:107
  19.3 6.6 %all-to-all-start = ((bf16[16,3,8,256]{3,2,1,0:T(8,128)(2,1)}), bf16[16,3,8,256]{3,2,1,0:T(8,128)(2,1)S(1)}, u32[]{:S(2)}, u32[]{:S(2)}) async-start(bf16[16,3,8,256]{3,2,1,0:T(8,128)(2,1)} %pad_maximum_fusion.2), calls=%async_computation | async-start | bytes 393216 | tf_op jit(solution)/shard_map/all_to_all | solution.py:107
  26.0 0.7 copy.49
  26.8 8.6 %all-to-all-done = bf16[16,3,8,256]{3,2,1,0:T(8,128)(2,1)S(1)} async-done(((bf16[16,3,8,256]{3,2,1,0:T(8,128)(2,1)}), bf16[16,3,8,256]{3,2,1,0:T(8,128)(2,1)S(1)}, u32[]{:S(2)}, u32[]{:S(2)}) %all-to-all-start) | async-done | bytes 196640 | tf_op jit(solution)/shard_map/all_to_all | solution.py:107
  35.4 3.6 %all-to-all-start.1 = ((bf16[32,8,1024]{2,1,0:T(8,128)(2,1)}), bf16[32,8,1024]{2,1,0:T(8,128)(2,1)S(1)}, u32[]{:S(2)}, u32[]{:S(2)}) async-start(bf16[32,8,1024]{2,1,0:T(8,128)(2,1)} %param.7), calls=%async_computation.1 | async-start | bytes 1048576 | tf_op jit(solution)/shard_map/all_to_all | solution.py:107
  39.1 0.1 add_multiply_fusion.1
  39.3 0.1 fusion.2
  39.3 0.1 add_multiply_fusion
  39.5 9.1 %collective-permute-start = (bf16[2,128,256]{2,1,0:T(8,128)(2,1)S(1)}, bf16[2,128,256]{2,1,0:T(8,128)(2,1)S(1)}, u32[]{:S(2)}, u32[]{:S(2)}) collective-permute-start(bf16[2,128,256]{2,1,0:T(8,128)(2,1)S(1)} %bitcast.102), channel_id=1, source_target_pairs={{0,128},{128,256},{256,384},{384,0},{1,129},{129,257},{257,385},{3... | collective-permute-start | bytes 393224 | tf_op jit(solution)/shard_map/ppermute | solution.py:111
  48.6 2.9 %collective-permute-start.2 = (bf16[2,128,256]{2,1,0:T(8,128)(2,1)S(1)}, bf16[2,128,256]{2,1,0:T(8,128)(2,1)S(1)}, u32[]{:S(2)}, u32[]{:S(2)}) collective-permute-start(bf16[2,128,256]{2,1,0:T(8,128)(2,1)S(1)} %bitcast.101), channel_id=1, source_target_pairs={{0,384},{128,0},{256,128},{384,256},{1,385},{129,1},{257,129},{385... | collective-permute-start | bytes 393224 | tf_op jit(solution)/shard_map/ppermute | solution.py:111
  51.5 10.8 %collective-permute-start.1 = (bf16[2,128,256]{2,1,0:T(8,128)(2,1)S(1)}, bf16[2,128,256]{2,1,0:T(8,128)(2,1)S(1)}, u32[]{:S(2)}, u32[]{:S(2)}) collective-permute-start(bf16[2,128,256]{2,1,0:T(8,128)(2,1)S(1)} %bitcast.100), channel_id=1, source_target_pairs={{0,256},{128,384},{256,0},{384,128},{1,257},{129,385},{257,1},{385... | collective-permute-start | bytes 393224 | tf_op jit(solution)/shard_map/ppermute | solution.py:111
  62.3 0.1 pad_add_fusion.where_ref
  62.4 0.3 convert_reduce_fusion.1
  62.7 10.1 %collective-permute-done = bf16[2,128,256]{2,1,0:T(8,128)(2,1)S(1)} collective-permute-done((bf16[2,128,256]{2,1,0:T(8,128)(2,1)S(1)}, bf16[2,128,256]{2,1,0:T(8,128)(2,1)S(1)}, u32[]{:S(2)}, u32[]{:S(2)}) %collective-permute-start) | collective-permute-done | bytes 131104 | tf_op jit(solution)/shard_map/ppermute | solution.py:111
  72.8 6.3 %collective-permute-done.1 = bf16[2,128,256]{2,1,0:T(8,128)(2,1)S(1)} collective-permute-done((bf16[2,128,256]{2,1,0:T(8,128)(2,1)S(1)}, bf16[2,128,256]{2,1,0:T(8,128)(2,1)S(1)}, u32[]{:S(2)}, u32[]{:S(2)}) %collective-permute-start.1) | collective-permute-done | bytes 131104 | tf_op jit(solution)/shard_map/ppermute | solution.py:111
  79.2 5.8 %shard_map.86 = (bf16[4,2,128,1024]{3,2,1,0:T(8,128)(2,1)S(1)}, f32[2,8,128]{2,1,0:T(8,128)S(1)}) custom-call(s32[2]{0:T(128)S(1)} %pad_add_fusion.where_ref, s32[1,128]{1,0:T(1,128)S(1)} %get-tuple-element.31.bounds_ref, bf16[2,128,1024]{2,1,0:T(8,128)(2,1)S(1)} %bitcast.89, bf16[4,2,128,256]{3,2,1,0:T(8,128)(2,1)S(1)} %pad_maximum_fusion.far_ref, ...), custom_call_target="tpu_custom_call" | custom-call | flops 671088640 | bytes 2097152 | tf_op jit(solution)/shard_map/pallas_call | solution.py:68
  85.0 1.3 copy-done.1
  86.3 6.0 %all-to-all-start.2 = ((bf16[4,256,1024]{2,1,0:T(8,128)(2,1)}), bf16[4,256,1024]{2,1,0:T(8,128)(2,1)S(1)}, u32[]{:S(2)}, u32[]{:S(2)}) async-start(bf16[4,256,1024]{2,1,0:T(8,128)(2,1)} %bitcast.88), calls=%async_computation.2 | async-start | bytes 4194304 | tf_op jit(solution)/shard_map/all_to_all | solution.py:107
  92.3 0.3 select_reduce_fusion
  92.6 0.1 broadcast_in_dim.58
  92.7 0.1 eq.68
  92.8 0.1 broadcast_in_dim.63
  92.8 0.1 eq.72
  93.0 5.3 %collective-permute-start.4 = (bf16[2,8,128]{2,1,0:T(8,128)(2,1)S(1)}, bf16[2,8,128]{2,1,0:T(8,128)(2,1)S(1)}, u32[]{:S(2)}, u32[]{:S(2)}) collective-permute-start(bf16[2,8,128]{2,1,0:T(8,128)(2,1)S(1)} %convert_element_type.37), channel_id=1, source_target_pairs={{0,256},{128,384},{256,0},{384,128},{1,257},{129,385},{257,1},{385... | collective-permute-start | bytes 12296 | tf_op jit(solution)/shard_map/ppermute | solution.py:111
  98.2 10.5 %collective-permute-start.3 = (bf16[2,8,128]{2,1,0:T(8,128)(2,1)S(1)}, bf16[2,8,128]{2,1,0:T(8,128)(2,1)S(1)}, u32[]{:S(2)}, u32[]{:S(2)}) collective-permute-start(bf16[2,8,128]{2,1,0:T(8,128)(2,1)S(1)} %convert_element_type.37), channel_id=1, source_target_pairs={{0,128},{128,256},{256,384},{384,0},{1,129},{129,257},{257,385},{3... | collective-permute-start | bytes 12296 | tf_op jit(solution)/shard_map/ppermute | solution.py:111
  108.8 1.9 %collective-permute-start.5 = (bf16[2,8,128]{2,1,0:T(8,128)(2,1)S(1)}, bf16[2,8,128]{2,1,0:T(8,128)(2,1)S(1)}, u32[]{:S(2)}, u32[]{:S(2)}) collective-permute-start(bf16[2,8,128]{2,1,0:T(8,128)(2,1)S(1)} %convert_element_type.37), channel_id=1, source_target_pairs={{0,384},{128,0},{256,128},{384,256},{1,385},{129,1},{257,129},{385... | collective-permute-start | bytes 12296 | tf_op jit(solution)/shard_map/ppermute | solution.py:111
  110.7 7.4 %collective-permute-done.5 = bf16[2,8,128]{2,1,0:T(8,128)(2,1)S(1)} collective-permute-done((bf16[2,8,128]{2,1,0:T(8,128)(2,1)S(1)}, bf16[2,8,128]{2,1,0:T(8,128)(2,1)S(1)}, u32[]{:S(2)}, u32[]{:S(2)}) %collective-permute-start.5) | collective-permute-done | bytes 4128 | tf_op jit(solution)/shard_map/ppermute | solution.py:111
  118.2 0.1 select_add_fusion
  118.3 2.9 %all-gather.2.cloned.1.call-done = bf16[16,8,8,1024]{3,2,0,1:T(8,128)(2,1)} async-done(((bf16[1,8,8,1024]{3,2,0,1:T(8,128)(2,1)}), bf16[16,8,8,1024]{3,2,0,1:T(8,128)(2,1)}) %all-gather.2.cloned.1.call-update) | async-done | bytes 2097168 | tf_op jit(solution)/shard_map/all_gather | solution.py:123
  121.2 1.6 copy-done
  122.7 1.2 shard_map.88
  124.0 1.9 %collective-permute-start.6 = (bf16[4,1024,128]{2,1,0:T(8,128)(2,1)S(1)}, bf16[4,1024,128]{2,1,0:T(8,128)(2,1)S(1)}, u32[]{:S(2)}, u32[]{:S(2)}) collective-permute-start(bf16[4,1024,128]{2,1,0:T(8,128)(2,1)S(1)} %shard_map.88), channel_id=1, source_target_pairs={{0,1},{1,0},{2,3},{3,2},{4,5},{5,4},{6,7},{7,6},{8,9},{9,8},{10,11... | collective-permute-start | bytes 3145736 | tf_op jit(solution)/shard_map/ppermute | solution.py:163
  125.9 1.2 shard_map.87
  127.2 1.4 collective-permute-done.6
  128.6 0.2 add_convert_fusion
  128.8 18.9 %all_to_all.43 = bf16[4,1024,128]{2,1,0:T(8,128)(2,1)S(1)} all-to-all(bf16[4,1024,128]{2,1,0:T(8,128)(2,1)S(1)} %add_convert_fusion), channel_id=1, replica_groups=mesh['za'=2,'zb'=2,'zl'=4,'x'=4,'y'=4,'c'=2] {'y'}, dimensions={0} | all-to-all | bytes 2097152 | tf_op jit(solution)/shard_map/all_to_all | solution.py:107
  147.6 0.3 reduce_sum.41
  147.9 0.8 copy.50
  148.8 5.8 %all-to-all-start.5 = ((bf16[16,12,8,128]{3,2,1,0:T(8,128)(2,1)}), bf16[16,12,8,128]{3,2,1,0:T(8,128)(2,1)S(1)}, u32[]{:S(2)}, u32[]{:S(2)}) async-start(bf16[16,12,8,128]{3,2,1,0:T(8,128)(2,1)} %copy.50), calls=%async_computation.5 | async-start | bytes 786432 | tf_op jit(solution)/shard_map/all_to_all | solution.py:107
  154.6 12.0 %all-to-all-done.5 = bf16[16,12,8,128]{3,2,1,0:T(8,128)(2,1)S(1)} async-done(((bf16[16,12,8,128]{3,2,1,0:T(8,128)(2,1)}), bf16[16,12,8,128]{3,2,1,0:T(8,128)(2,1)S(1)}, u32[]{:S(2)}, u32[]{:S(2)}) %all-to-all-start.5) | async-done | bytes 393248 | tf_op jit(solution)/shard_map/all_to_all | solution.py:107
  166.7 0.8 add_convert_fusion.1
  167.6 0.6 maximum_bitcast_fusion
  (42 shorter events, 0.7 us)
Async XLA Ops:
  8.2 31.1 %copy-start.3 = (s32[129]{0:T(256)S(1)}, s32[129]{0:T(256)}, u32[]{:S(2)}) copy-start(s32[129]{0:T(256)} %param.12) | copy-start | bytes 1552
  9.1 10.3 %all-to-all-start.3 = ((bf16[4,8,2,1024]{3,1,2,0:T(8,128)(2,1)}), bf16[4,8,2,1024]{3,1,2,0:T(8,128)(2,1)S(1)}, u32[]{:S(2)}, u32[]{:S(2)}) async-start(bf16[4,8,2,1024]{3,1,2,0:T(8,128)(2,1)} %reshape.150), calls=%async_computation.3 | async-start | bytes 262144 | tf_op jit(solution)/shard_map/all_to_all | solution.py:107
  19.3 16.1 %all-to-all-start = ((bf16[16,3,8,256]{3,2,1,0:T(8,128)(2,1)}), bf16[16,3,8,256]{3,2,1,0:T(8,128)(2,1)S(1)}, u32[]{:S(2)}, u32[]{:S(2)}) async-start(bf16[16,3,8,256]{3,2,1,0:T(8,128)(2,1)} %pad_maximum_fusion.2), calls=%async_computation | async-start | bytes 393216 | tf_op jit(solution)/shard_map/all_to_all | solution.py:107
  26.0 95.2 %all-gather.2.cloned.1.call-start = ((), (), s32[]{:S(2)}) async-start(), calls=%async_computation.6 | async-start | bytes 2228224 | tf_op jit(solution)/shard_map/all_gather | solution.py:123
  35.4 43.7 %all-to-all-start.1 = ((bf16[32,8,1024]{2,1,0:T(8,128)(2,1)}), bf16[32,8,1024]{2,1,0:T(8,128)(2,1)S(1)}, u32[]{:S(2)}, u32[]{:S(2)}) async-start(bf16[32,8,1024]{2,1,0:T(8,128)(2,1)} %param.7), calls=%async_computation.1 | async-start | bytes 1048576 | tf_op jit(solution)/shard_map/all_to_all | solution.py:107
  39.5 33.3 %collective-permute-start = (bf16[2,128,256]{2,1,0:T(8,128)(2,1)S(1)}, bf16[2,128,256]{2,1,0:T(8,128)(2,1)S(1)}, u32[]{:S(2)}, u32[]{:S(2)}) collective-permute-start(bf16[2,128,256]{2,1,0:T(8,128)(2,1)S(1)} %bitcast.102), channel_id=1, source_target_pairs={{0,128},{128,256},{256,384},{384,0},{1,129},{129,257},{257,385},{3... | collective-permute-start | bytes 393224 | tf_op jit(solution)/shard_map/ppermute | solution.py:111
  48.6 24.2 %collective-permute-start.2 = (bf16[2,128,256]{2,1,0:T(8,128)(2,1)S(1)}, bf16[2,128,256]{2,1,0:T(8,128)(2,1)S(1)}, u32[]{:S(2)}, u32[]{:S(2)}) collective-permute-start(bf16[2,128,256]{2,1,0:T(8,128)(2,1)S(1)} %bitcast.101), channel_id=1, source_target_pairs={{0,384},{128,0},{256,128},{384,256},{1,385},{129,1},{257,129},{385... | collective-permute-start | bytes 393224 | tf_op jit(solution)/shard_map/ppermute | solution.py:111
  51.5 27.6 %collective-permute-start.1 = (bf16[2,128,256]{2,1,0:T(8,128)(2,1)S(1)}, bf16[2,128,256]{2,1,0:T(8,128)(2,1)S(1)}, u32[]{:S(2)}, u32[]{:S(2)}) collective-permute-start(bf16[2,128,256]{2,1,0:T(8,128)(2,1)S(1)} %bitcast.100), channel_id=1, source_target_pairs={{0,256},{128,384},{256,0},{384,128},{1,257},{129,385},{257,1},{385... | collective-permute-start | bytes 393224 | tf_op jit(solution)/shard_map/ppermute | solution.py:111
  85.0 1.3 copy-start.1
  86.3 6.0 %copy-start.4 = (s32[128]{0:T(128)S(1)}, s32[128]{0:T(128)}, u32[]{:S(2)}) copy-start(s32[128]{0:T(128)} %param.13) | copy-start | bytes 1540
  86.3 32.0 %all-to-all-start.2 = ((bf16[4,256,1024]{2,1,0:T(8,128)(2,1)}), bf16[4,256,1024]{2,1,0:T(8,128)(2,1)S(1)}, u32[]{:S(2)}, u32[]{:S(2)}) async-start(bf16[4,256,1024]{2,1,0:T(8,128)(2,1)} %bitcast.88), calls=%async_computation.2 | async-start | bytes 4194304 | tf_op jit(solution)/shard_map/all_to_all | solution.py:107
  93.0 17.7 %collective-permute-start.4 = (bf16[2,8,128]{2,1,0:T(8,128)(2,1)S(1)}, bf16[2,8,128]{2,1,0:T(8,128)(2,1)S(1)}, u32[]{:S(2)}, u32[]{:S(2)}) collective-permute-start(bf16[2,8,128]{2,1,0:T(8,128)(2,1)S(1)} %convert_element_type.37), channel_id=1, source_target_pairs={{0,256},{128,384},{256,0},{384,128},{1,257},{129,385},{257,1},{385... | collective-permute-start | bytes 12296 | tf_op jit(solution)/shard_map/ppermute | solution.py:111
  98.2 12.5 %collective-permute-start.3 = (bf16[2,8,128]{2,1,0:T(8,128)(2,1)S(1)}, bf16[2,8,128]{2,1,0:T(8,128)(2,1)S(1)}, u32[]{:S(2)}, u32[]{:S(2)}) collective-permute-start(bf16[2,8,128]{2,1,0:T(8,128)(2,1)S(1)} %convert_element_type.37), channel_id=1, source_target_pairs={{0,128},{128,256},{256,384},{384,0},{1,129},{129,257},{257,385},{3... | collective-permute-start | bytes 12296 | tf_op jit(solution)/shard_map/ppermute | solution.py:111
  108.8 9.4 %collective-permute-start.5 = (bf16[2,8,128]{2,1,0:T(8,128)(2,1)S(1)}, bf16[2,8,128]{2,1,0:T(8,128)(2,1)S(1)}, u32[]{:S(2)}, u32[]{:S(2)}) collective-permute-start(bf16[2,8,128]{2,1,0:T(8,128)(2,1)S(1)} %convert_element_type.37), channel_id=1, source_target_pairs={{0,384},{128,0},{256,128},{384,256},{1,385},{129,1},{257,129},{385... | collective-permute-start | bytes 12296 | tf_op jit(solution)/shard_map/ppermute | solution.py:111
  121.2 1.6 copy-start
  124.0 4.6 %collective-permute-start.6 = (bf16[4,1024,128]{2,1,0:T(8,128)(2,1)S(1)}, bf16[4,1024,128]{2,1,0:T(8,128)(2,1)S(1)}, u32[]{:S(2)}, u32[]{:S(2)}) collective-permute-start(bf16[4,1024,128]{2,1,0:T(8,128)(2,1)S(1)} %shard_map.88), channel_id=1, source_target_pairs={{0,1},{1,0},{2,3},{3,2},{4,5},{5,4},{6,7},{7,6},{8,9},{9,8},{10,11... | collective-permute-start | bytes 3145736 | tf_op jit(solution)/shard_map/ppermute | solution.py:163
  147.9 18.8 %copy-start.2 = (bf16[32,8,512]{2,1,0:T(8,128)(2,1)S(1)}, bf16[32,8,512]{2,1,0:T(8,128)(2,1)}, u32[]{:S(2)}) copy-start(bf16[32,8,512]{2,1,0:T(8,128)(2,1)} %param.10) | copy-start | bytes 786436
  148.8 17.8 %all-to-all-start.5 = ((bf16[16,12,8,128]{3,2,1,0:T(8,128)(2,1)}), bf16[16,12,8,128]{3,2,1,0:T(8,128)(2,1)S(1)}, u32[]{:S(2)}, u32[]{:S(2)}) async-start(bf16[16,12,8,128]{3,2,1,0:T(8,128)(2,1)} %copy.50), calls=%async_computation.5 | async-start | bytes 786432 | tf_op jit(solution)/shard_map/all_to_all | solution.py:107
Sparse Core Ops, SparseCore 0:
  28.9 92.2 all-gather.1

commit v3 on v2

--- a/solution.py
+++ b/solution.py
@@ -80,27 +80,52 @@
     )(where, bounds, query, far, near)
 
 
-def project_kernel(rows_ref, weight_ref, out_ref):
-    for part in range(4):
-        rows = slice(part * 256, (part + 1) * 256)
-        product = jnp.dot(rows_ref[rows], weight_ref[...], preferred_element_type=jnp.float32)
-        for y in range(4):
-            out_ref[y, rows] = product[:, y * 128 : (y + 1) * 128].astype(out_ref.dtype)
-
-
-def project(rows, weight, half, dtype):
-    vmem = pl.BlockSpec(memory_space=pltpu.VMEM)
+def project_kernel(core_ref, own_ref, other_ref, own_weight_ref, other_weight_ref, out_ref):
+    del core_ref
+    product = jnp.dot(own_ref[...], own_weight_ref[...], preferred_element_type=jnp.float32)
+    product += jnp.dot(other_ref[...], other_weight_ref[...], preferred_element_type=jnp.float32)
+    for y in range(4):
+        out_ref[y] = product[:, y * 128 : (y + 1) * 128].astype(out_ref.dtype)
+
+
+def project(core, own, other, weight):
+    rows = pl.BlockSpec((512, 1024), lambda i, core: (i, 0))
     return pl.pallas_call(
         project_kernel,
-        grid=(1,),
-        out_shape=jax.ShapeDtypeStruct((4, 1024, 128), dtype),
-        in_specs=[vmem, pl.BlockSpec((1024, 512), lambda i: (0, half))],
-        out_specs=vmem,
+        grid_spec=pltpu.PrefetchScalarGridSpec(
+            num_scalar_prefetch=1,
+            grid=(2,),
+            in_specs=[
+                rows,
+                rows,
+                pl.BlockSpec((1024, 512), lambda i, core: (core[0], 0)),
+                pl.BlockSpec((1024, 512), lambda i, core: (1 - core[0], 0)),
+            ],
+            out_specs=pl.BlockSpec((4, 512, 128), lambda i, core: (0, i, 0)),
+        ),
+        out_shape=jax.ShapeDtypeStruct((4, 1024, 128), jnp.bfloat16),
         compiler_params=pltpu.CompilerParams(vmem_limit_bytes=32 * 1024 * 1024),
         cost_estimate=pl.CostEstimate(
-            flops=2 * 1024 * 1024 * 512, bytes_accessed=4 * 1024 * 1024, transcendentals=0
-        ),
-    )(rows, weight)
+            flops=2 * 1024 * 2048 * 512, bytes_accessed=7 * 1024 * 1024, transcendentals=0
+        ),
+    )(core.reshape(1), own, other, weight, weight)
+
+
+def arrange_kernel(source_ref, out_ref):
+    for k in range(out_ref.shape[0]):
+        out_ref[k] = source_ref[:, k]
+
+
+def arrange(source):
+    return pl.pallas_call(
+        arrange_kernel,
+        grid=(4,),
+        out_shape=jax.ShapeDtypeStruct(source.shape, source.dtype),
+        in_specs=[pl.BlockSpec((16, 4, 8, 512), lambda i: (0, i, 0, 0))],
+        out_specs=pl.BlockSpec((4, 16, 8, 512), lambda i: (i, 0, 0, 0)),
+        compiler_params=pltpu.CompilerParams(vmem_limit_bytes=32 * 1024 * 1024),
+        cost_estimate=pl.CostEstimate(flops=10**11, bytes_accessed=4 * 1024 * 1024, transcendentals=0),
+    )(source)
 
 
 def swap(source, axes, split=0, concat=0):
@@ -117,17 +142,17 @@
     core = lax.axis_index("c")
     beta = 4 * zl + x
 
-    weight = out_weight.reshape(8, 2, 4, 2, 4, 128)
-    weight = jnp.where(core == 0, weight, jnp.flip(weight, 3)).transpose(4, 0, 1, 3, 2, 5).reshape(4, 8, 2, 1024)
-    weight = swap(weight, "x").transpose(1, 0, 2, 3).reshape(8, 8, 1024)
+    weight = out_weight.reshape(8, 2, 4, 2, 4, 128).transpose(4, 3, 0, 1, 2, 5).reshape(8, 16, 512)
+    weight = swap(weight, ("x", "c")).reshape(4, 2, 8, 2, 512)
+    weight = weight.transpose(1, 2, 0, 3, 4).reshape(16, 8, 512)
+    weight, key_rows, value_rows = lax.optimization_barrier((weight, key_rows, value_rows))
     gathered = lax.all_gather(weight, Z, axis=0, tiled=False)
-    gathered = gathered.transpose(1, 0, 2, 3).reshape(1024, 1024)
+    gathered = arrange(gathered).reshape(2048, 512)
 
     both = jnp.concatenate([key_rows, value_rows], axis=2)
     pairs = both.reshape(16, 2, 8, 256)
     before = jnp.concatenate([pairs[:1, 1:], pairs[:-1, 1:]], axis=0)
-    near3, weight = lax.optimization_barrier((jnp.concatenate([before, pairs], axis=1), weight))
-    near3 = swap(near3, NEAR)
+    near3 = swap(jnp.concatenate([before, pairs], axis=1), NEAR)
     near3 = near3.transpose(1, 0, 2, 3).reshape(3, ROWS, 256)
 
     far = [near3[:2]]
@@ -159,11 +184,8 @@
 
     wide = swap(attended.reshape(4, 256, 1024), "x").reshape(1024, 1024)
     wide, packed = lax.optimization_barrier((wide, packed))
-    theirs = project(wide, gathered, 1, bf16)
-    got = lax.ppermute(theirs, "c", [(0, 1), (1, 0)])
-    ours = project(wide, gathered, 0, f32)
-    ours, got = lax.optimization_barrier((ours, got))
-    parts = swap((ours + got.astype(f32)).astype(bf16), "y")
+    other = shift(wide, "c", 2, 1)
+    parts = swap(project(core.astype(i32), wide, other, gathered), "y")
     summed = jnp.sum(parts.astype(f32), axis=0).astype(bf16)
     summed = summed.reshape(8, 16, 8, 128).transpose(1, 0, 2, 3)
     home = swap(jnp.concatenate([summed, packed], axis=1), NEAR)

time: 176 us -> 185 us (1.051)
  blocking collectives: 18.9 us -> 28.7 us
  starting transfers between devices: 68.7 us -> 64.3 us
  local copies, waits for them, and re-layouts: 6.88 us -> 10.3 us
    all_to_all x1 -> x2, blocking collectives: 18.9 us -> 28.7 us  [swap(): lax.all_to_all(source, axes, split_axis=split, concat_axis=concat, tiled=...]
    all_to_all x5 -> x4, starting transfers between devices: 26.2 us -> 20.6 us  [swap(): lax.all_to_all(source, axes, split_axis=split, concat_axis=concat, tiled=...]
    all_to_all x5 -> x4, waiting for transfers between devices: 25 us -> 20.7 us  [swap(): lax.all_to_all(source, axes, split_axis=split, concat_axis=concat, tiled=...]
    all_gather x0 -> x1, local copies, waits for them, and re-layouts: none -> 4.11 us  [local(): gathered = lax.all_gather(weight, Z, axis=0, tiled=False)]
    ppermute x6 -> x7, starting transfers between devices: 40.5 us -> 43.6 us  [shift(): lax.ppermute(source, axes, [(i, (i + step) % size) for i in range(size)])]
    ppermute x6 -> x7, waiting for transfers between devices: 23.8 us -> 26.8 us  [shift(): lax.ppermute(source, axes, [(i, (i + step) % size) for i in range(size)])]
    ppermute x1 -> x0, starting transfers between devices: 1.92 us -> none  [local(): got = lax.ppermute(theirs, 'c', [(0, 1), (1, 0)])]
    all_gather x1, waiting for transfers between devices: 2.88 us -> 4.74 us  [local(): gathered = lax.all_gather(weight, Z, axis=0, tiled=False)]
  transfers between devices with their start and end apart: 13 -> 12, of which waited for: 8 -> 7; matrix products, arithmetic and copies ran while one was open for 2% -> 3% of each run, Pallas kernels for 4% -> 3%
where the time goes in v3:
time: 185 us; the launch traced here: 184 us
  starting transfers between devices  64.3 us (35%)
  waiting for transfers between devices  52.9 us (29%)
  blocking collectives  28.7 us (16%)
  between operations  14.5 us (8%)
  local copies, waits for them, and re-layouts  10.3 us (6%)
  Pallas kernels  8.76 us (5%)
  other arithmetic  4.44 us (2%)
    ppermute x7, starting transfers between devices, shift(): lax.ppermute(source, axes, [(i, (i + step) % size) for i in range(size)])  43.6 us
    all_to_all x2, blocking collectives, swap(): lax.all_to_all(source, axes, split_axis=split, concat_axis=concat, tiled=...  28.7 us
    ppermute x7, waiting for transfers between devices, shift(): lax.ppermute(source, axes, [(i, (i + step) % size) for i in range(size)])  26.8 us
    all_to_all x4, waiting for transfers between devices, swap(): lax.all_to_all(source, axes, split_axis=split, concat_axis=concat, tiled=...  20.7 us
    all_to_all x4, starting transfers between devices, swap(): lax.all_to_all(source, axes, split_axis=split, concat_axis=concat, tiled=...  20.6 us
    pallas_call x1, Pallas kernels, attend(): pl.pallas_call(attend_kernel, out_shape=(jax.ShapeDtypeStruct((4, 2, ROWS...  5.82 us
    all_gather x1, waiting for transfers between devices, local(): gathered = lax.all_gather(weight, Z, axis=0, tiled=False)  4.74 us
    all_gather x1, local copies, waits for them, and re-layouts, local(): gathered = lax.all_gather(weight, Z, axis=0, tiled=False)  4.11 us
  transfers between devices with their start and end apart: 12, of which 7 were waited for; matrix products, arithmetic and copies ran while one was open for 3% of the time, Pallas kernels for 3%

profile of v3, /device:TPU:8, one launch (start us, length us, event | category | flops | bytes accessed | tf_op | source)
XLA Modules:
  0.0 183.9 jit_solution(11528434226036966803)
XLA Ops:
  7.2 1.0 reshape.154
  8.3 10.2 %all_to_all.43 = bf16[8,16,512]{2,1,0:T(8,128)(2,1)S(1)} all-to-all(bf16[8,16,512]{2,1,0:T(8,128)(2,1)S(1)} %reshape.155), channel_id=1, replica_groups=mesh['za'=2,'zb'=2,'zl'=4,'x'=4,'y'=4,'c'=2] {'x','c'}, dimensions={0} | all-to-all | bytes 262144 | tf_op jit(solution)/shard_map/all_to_all | solution.py:132
  18.6 0.7 copy.40
  19.3 0.9 pad_maximum_fusion.3
  20.2 0.7 pad_maximum_fusion.2
  20.9 6.6 %all-to-all-start.1 = ((bf16[16,3,8,256]{3,2,1,0:T(8,128)(2,1)}), bf16[16,3,8,256]{3,2,1,0:T(8,128)(2,1)S(1)}, u32[]{:S(2)}, u32[]{:S(2)}) async-start(bf16[16,3,8,256]{3,2,1,0:T(8,128)(2,1)} %pad_maximum_fusion.2), calls=%async_computation.1 | async-start | bytes 393216 | tf_op jit(solution)/shard_map/all_to_all | solution.py:132
  27.6 0.7 all-gather.3.cloned.1.call-update
  28.3 8.7 %all-to-all-done.1 = bf16[16,3,8,256]{3,2,1,0:T(8,128)(2,1)S(1)} async-done(((bf16[16,3,8,256]{3,2,1,0:T(8,128)(2,1)}), bf16[16,3,8,256]{3,2,1,0:T(8,128)(2,1)S(1)}, u32[]{:S(2)}, u32[]{:S(2)}) %all-to-all-start.1) | async-done | bytes 196640 | tf_op jit(solution)/shard_map/all_to_all | solution.py:132
  37.0 3.6 %all-to-all-start.2 = ((bf16[32,8,1024]{2,1,0:T(8,128)(2,1)}), bf16[32,8,1024]{2,1,0:T(8,128)(2,1)S(1)}, u32[]{:S(2)}, u32[]{:S(2)}) async-start(bf16[32,8,1024]{2,1,0:T(8,128)(2,1)} %param.7), calls=%async_computation.2 | async-start | bytes 1048576 | tf_op jit(solution)/shard_map/all_to_all | solution.py:132
  40.7 0.1 add_multiply_fusion.1
  40.8 0.1 iota_add_fusion
  40.8 0.1 fusion.1
  40.9 0.1 add_multiply_fusion
  41.1 9.1 %collective-permute-start = (bf16[2,128,256]{2,1,0:T(8,128)(2,1)S(1)}, bf16[2,128,256]{2,1,0:T(8,128)(2,1)S(1)}, u32[]{:S(2)}, u32[]{:S(2)}) collective-permute-start(bf16[2,128,256]{2,1,0:T(8,128)(2,1)S(1)} %bitcast.103), channel_id=1, source_target_pairs={{0,128},{128,256},{256,384},{384,0},{1,129},{129,257},{257,385},{3... | collective-permute-start | bytes 393224 | tf_op jit(solution)/shard_map/ppermute | solution.py:136
  50.2 2.9 %collective-permute-start.2 = (bf16[2,128,256]{2,1,0:T(8,128)(2,1)S(1)}, bf16[2,128,256]{2,1,0:T(8,128)(2,1)S(1)}, u32[]{:S(2)}, u32[]{:S(2)}) collective-permute-start(bf16[2,128,256]{2,1,0:T(8,128)(2,1)S(1)} %bitcast.102), channel_id=1, source_target_pairs={{0,384},{128,0},{256,128},{384,256},{1,385},{129,1},{257,129},{385... | collective-permute-start | bytes 393224 | tf_op jit(solution)/shard_map/ppermute | solution.py:136
  53.0 10.8 %collective-permute-start.1 = (bf16[2,128,256]{2,1,0:T(8,128)(2,1)S(1)}, bf16[2,128,256]{2,1,0:T(8,128)(2,1)S(1)}, u32[]{:S(2)}, u32[]{:S(2)}) collective-permute-start(bf16[2,128,256]{2,1,0:T(8,128)(2,1)S(1)} %bitcast.101), channel_id=1, source_target_pairs={{0,256},{128,384},{256,0},{384,128},{1,257},{129,385},{257,1},{385... | collective-permute-start | bytes 393224 | tf_op jit(solution)/shard_map/ppermute | solution.py:136
  63.9 0.1 pad_add_fusion.where_ref
  63.9 0.3 convert_reduce_fusion.1
  64.3 13.7 %collective-permute-done = bf16[2,128,256]{2,1,0:T(8,128)(2,1)S(1)} collective-permute-done((bf16[2,128,256]{2,1,0:T(8,128)(2,1)S(1)}, bf16[2,128,256]{2,1,0:T(8,128)(2,1)S(1)}, u32[]{:S(2)}, u32[]{:S(2)}) %collective-permute-start) | collective-permute-done | bytes 131104 | tf_op jit(solution)/shard_map/ppermute | solution.py:136
  78.0 3.4 %collective-permute-done.1 = bf16[2,128,256]{2,1,0:T(8,128)(2,1)S(1)} collective-permute-done((bf16[2,128,256]{2,1,0:T(8,128)(2,1)S(1)}, bf16[2,128,256]{2,1,0:T(8,128)(2,1)S(1)}, u32[]{:S(2)}, u32[]{:S(2)}) %collective-permute-start.1) | collective-permute-done | bytes 131104 | tf_op jit(solution)/shard_map/ppermute | solution.py:136
  81.4 0.1 pad_maximum_fusion.far_ref
  81.6 5.8 %shard_map.86 = (bf16[4,2,128,1024]{3,2,1,0:T(8,128)(2,1)S(1)}, f32[2,8,128]{2,1,0:T(8,128)S(1)}) custom-call(s32[2]{0:T(128)S(1)} %pad_add_fusion.where_ref, s32[1,128]{1,0:T(1,128)S(1)} %get-tuple-element.33.bounds_ref, bf16[2,128,1024]{2,1,0:T(8,128)(2,1)S(1)} %bitcast.88, bf16[4,2,128,256]{3,2,1,0:T(8,128)(2,1)S(1)} %pad_maximum_fusion.far_ref, ...), custom_call_target="tpu_custom_call" | custom-call | flops 671088640 | bytes 2097152 | tf_op jit(solution)/shard_map/pallas_call | solution.py:68
  87.4 1.3 copy-done
  88.7 5.1 %all-to-all-start.3 = ((bf16[4,256,1024]{2,1,0:T(8,128)(2,1)}), bf16[4,256,1024]{2,1,0:T(8,128)(2,1)S(1)}, u32[]{:S(2)}, u32[]{:S(2)}) async-start(bf16[4,256,1024]{2,1,0:T(8,128)(2,1)} %bitcast.86), calls=%async_computation.3 | async-start | bytes 4194304 | tf_op jit(solution)/shard_map/all_to_all | solution.py:132
  93.9 0.3 select_reduce_fusion
  94.2 0.1 broadcast_in_dim.58
  94.2 0.1 eq.65
  94.3 0.1 broadcast_in_dim.63
  94.4 0.1 eq.69
  94.5 7.4 %collective-permute-start.4 = (bf16[2,8,128]{2,1,0:T(8,128)(2,1)S(1)}, bf16[2,8,128]{2,1,0:T(8,128)(2,1)S(1)}, u32[]{:S(2)}, u32[]{:S(2)}) collective-permute-start(bf16[2,8,128]{2,1,0:T(8,128)(2,1)S(1)} %convert_element_type.31), channel_id=1, source_target_pairs={{0,256},{128,384},{256,0},{384,128},{1,257},{129,385},{257,1},{385... | collective-permute-start | bytes 12296 | tf_op jit(solution)/shard_map/ppermute | solution.py:136
  102.0 9.6 %collective-permute-start.3 = (bf16[2,8,128]{2,1,0:T(8,128)(2,1)S(1)}, bf16[2,8,128]{2,1,0:T(8,128)(2,1)S(1)}, u32[]{:S(2)}, u32[]{:S(2)}) collective-permute-start(bf16[2,8,128]{2,1,0:T(8,128)(2,1)S(1)} %convert_element_type.31), channel_id=1, source_target_pairs={{0,128},{128,256},{256,384},{384,0},{1,129},{129,257},{257,385},{3... | collective-permute-start | bytes 12296 | tf_op jit(solution)/shard_map/ppermute | solution.py:136
  111.6 1.9 %collective-permute-start.5 = (bf16[2,8,128]{2,1,0:T(8,128)(2,1)S(1)}, bf16[2,8,128]{2,1,0:T(8,128)(2,1)S(1)}, u32[]{:S(2)}, u32[]{:S(2)}) collective-permute-start(bf16[2,8,128]{2,1,0:T(8,128)(2,1)S(1)} %convert_element_type.31), channel_id=1, source_target_pairs={{0,384},{128,0},{256,128},{384,256},{1,385},{129,1},{257,129},{385... | collective-permute-start | bytes 12296 | tf_op jit(solution)/shard_map/ppermute | solution.py:136
  113.5 7.5 %collective-permute-done.5 = bf16[2,8,128]{2,1,0:T(8,128)(2,1)S(1)} collective-permute-done((bf16[2,8,128]{2,1,0:T(8,128)(2,1)S(1)}, bf16[2,8,128]{2,1,0:T(8,128)(2,1)S(1)}, u32[]{:S(2)}, u32[]{:S(2)}) %collective-permute-start.5) | collective-permute-done | bytes 4128 | tf_op jit(solution)/shard_map/ppermute | solution.py:136
  121.0 0.1 select_add_fusion
  121.1 4.7 %all-gather.3.cloned.1.call-done = bf16[256,8,512]{2,0,1:T(8,128)(2,1)} async-done(((bf16[16,8,512]{2,0,1:T(8,128)(2,1)}), bf16[256,8,512]{2,0,1:T(8,128)(2,1)}) %all-gather.3.cloned.1.call-update) | async-done | bytes 2097168 | tf_op jit(solution)/shard_map/all_gather | solution.py:149
  125.8 4.1 %copy.47 = bf16[256,8,512]{2,1,0:T(8,128)(2,1)} copy(bf16[256,8,512]{2,0,1:T(8,128)(2,1)} %all-gather.3.cloned.1.call-done) | data formatting | bytes 4194304 | tf_op jit(solution)/shard_map/all_gather | solution.py:149
  130.0 1.9 %collective-permute-start.6 = (bf16[1024,1024]{1,0:T(8,128)(2,1)S(1)}, bf16[1024,1024]{1,0:T(8,128)(2,1)S(1)}, u32[]{:S(2)}, u32[]{:S(2)}) collective-permute-start(bf16[1024,1024]{1,0:T(8,128)(2,1)S(1)} %bitcast.84), channel_id=1, source_target_pairs={{0,1},{1,0},{2,3},{3,2},{4,5},{5,4},{6,7},{7,6},{8,9},{9,8},{10,11... | collective-permute-start | bytes 6291464 | tf_op jit(solution)/shard_map/ppermute | solution.py:136
  131.9 1.6 copy-done.1
  133.5 0.4 shard_map.87
  133.8 2.2 %collective-permute-done.6.other_ref = bf16[1024,1024]{1,0:T(8,128)(2,1)S(1)} collective-permute-done((bf16[1024,1024]{1,0:T(8,128)(2,1)S(1)}, bf16[1024,1024]{1,0:T(8,128)(2,1)S(1)}, u32[]{:S(2)}, u32[]{:S(2)}) %collective-permute-start.6) | collective-permute-done | bytes 2097184 | tf_op jit(solution)/shard_map/ppermute | solution.py:136
  136.0 2.6 %shard_map.88 = bf16[4,1024,128]{2,1,0:T(8,128)(2,1)S(1)} custom-call(s32[1]{0:T(128)} %bitcast.core_ref, bf16[1024,1024]{1,0:T(8,128)(2,1)S(1)} %bitcast.85, bf16[1024,1024]{1,0:T(8,128)(2,1)S(1)} %collective-permute-done.6.other_ref, bf16[2048,512]{1,0:T(8,128)(2,1)S(1)} %bitcast.82, bf16[2048,512]{1,0:T(8,128)(2,1)S(1)} %bitcast.83), custom_call_target="tpu_custom_call" | custom-call | flops 2147483648 | bytes 7340032 | tf_op jit(solution)/shard_map/pallas_call | solution.py:93
  138.6 18.4 %all_to_all.44 = bf16[4,1024,128]{2,1,0:T(8,128)(2,1)S(1)} all-to-all(bf16[4,1024,128]{2,1,0:T(8,128)(2,1)S(1)} %shard_map.88), channel_id=1, replica_groups=mesh['za'=2,'zb'=2,'zl'=4,'x'=4,'y'=4,'c'=2] {'y'}, dimensions={0} | all-to-all | bytes 2097152 | tf_op jit(solution)/shard_map/all_to_all | solution.py:132
  157.0 0.3 reduce_sum.41
  157.3 0.8 copy.48
  158.2 5.3 %all-to-all-start.5 = ((bf16[16,12,8,128]{3,2,1,0:T(8,128)(2,1)}), bf16[16,12,8,128]{3,2,1,0:T(8,128)(2,1)S(1)}, u32[]{:S(2)}, u32[]{:S(2)}) async-start(bf16[16,12,8,128]{3,2,1,0:T(8,128)(2,1)} %copy.48), calls=%async_computation.5 | async-start | bytes 786432 | tf_op jit(solution)/shard_map/all_to_all | solution.py:132
  163.5 12.0 %all-to-all-done.5 = bf16[16,12,8,128]{3,2,1,0:T(8,128)(2,1)S(1)} async-done(((bf16[16,12,8,128]{3,2,1,0:T(8,128)(2,1)}), bf16[16,12,8,128]{3,2,1,0:T(8,128)(2,1)S(1)}, u32[]{:S(2)}, u32[]{:S(2)}) %all-to-all-start.5) | async-done | bytes 393248 | tf_op jit(solution)/shard_map/all_to_all | solution.py:132
  175.6 0.8 add_convert_fusion
  176.4 0.6 maximum_bitcast_fusion
  (41 shorter events, 0.6 us)
Async XLA Ops:
  8.2 32.6 %copy-start.3 = (s32[129]{0:T(256)S(1)}, s32[129]{0:T(256)}, u32[]{:S(2)}) copy-start(s32[129]{0:T(256)} %param.12) | copy-start | bytes 1552
  20.9 16.1 %all-to-all-start.1 = ((bf16[16,3,8,256]{3,2,1,0:T(8,128)(2,1)}), bf16[16,3,8,256]{3,2,1,0:T(8,128)(2,1)S(1)}, u32[]{:S(2)}, u32[]{:S(2)}) async-start(bf16[16,3,8,256]{3,2,1,0:T(8,128)(2,1)} %pad_maximum_fusion.2), calls=%async_computation.1 | async-start | bytes 393216 | tf_op jit(solution)/shard_map/all_to_all | solution.py:132
  27.5 98.3 %all-gather.3.cloned.1.call-start = ((), (), s32[]{:S(2)}) async-start(), calls=%async_computation.6 | async-start | bytes 2228224 | tf_op jit(solution)/shard_map/all_gather | solution.py:149
  37.0 44.5 %all-to-all-start.2 = ((bf16[32,8,1024]{2,1,0:T(8,128)(2,1)}), bf16[32,8,1024]{2,1,0:T(8,128)(2,1)S(1)}, u32[]{:S(2)}, u32[]{:S(2)}) async-start(bf16[32,8,1024]{2,1,0:T(8,128)(2,1)} %param.7), calls=%async_computation.2 | async-start | bytes 1048576 | tf_op jit(solution)/shard_map/all_to_all | solution.py:132
  41.1 36.9 %collective-permute-start = (bf16[2,128,256]{2,1,0:T(8,128)(2,1)S(1)}, bf16[2,128,256]{2,1,0:T(8,128)(2,1)S(1)}, u32[]{:S(2)}, u32[]{:S(2)}) collective-permute-start(bf16[2,128,256]{2,1,0:T(8,128)(2,1)S(1)} %bitcast.103), channel_id=1, source_target_pairs={{0,128},{128,256},{256,384},{384,0},{1,129},{129,257},{257,385},{3... | collective-permute-start | bytes 393224 | tf_op jit(solution)/shard_map/ppermute | solution.py:136
  50.2 27.8 %collective-permute-start.2 = (bf16[2,128,256]{2,1,0:T(8,128)(2,1)S(1)}, bf16[2,128,256]{2,1,0:T(8,128)(2,1)S(1)}, u32[]{:S(2)}, u32[]{:S(2)}) collective-permute-start(bf16[2,128,256]{2,1,0:T(8,128)(2,1)S(1)} %bitcast.102), channel_id=1, source_target_pairs={{0,384},{128,0},{256,128},{384,256},{1,385},{129,1},{257,129},{385... | collective-permute-start | bytes 393224 | tf_op jit(solution)/shard_map/ppermute | solution.py:136
  53.0 28.4 %collective-permute-start.1 = (bf16[2,128,256]{2,1,0:T(8,128)(2,1)S(1)}, bf16[2,128,256]{2,1,0:T(8,128)(2,1)S(1)}, u32[]{:S(2)}, u32[]{:S(2)}) collective-permute-start(bf16[2,128,256]{2,1,0:T(8,128)(2,1)S(1)} %bitcast.101), channel_id=1, source_target_pairs={{0,256},{128,384},{256,0},{384,128},{1,257},{129,385},{257,1},{385... | collective-permute-start | bytes 393224 | tf_op jit(solution)/shard_map/ppermute | solution.py:136
  87.4 1.3 copy-start
  88.7 5.1 %copy-start.4 = (s32[128]{0:T(128)S(1)}, s32[128]{0:T(128)}, u32[]{:S(2)}) copy-start(s32[128]{0:T(128)} %param.13) | copy-start | bytes 1540
  88.7 41.2 %all-to-all-start.3 = ((bf16[4,256,1024]{2,1,0:T(8,128)(2,1)}), bf16[4,256,1024]{2,1,0:T(8,128)(2,1)S(1)}, u32[]{:S(2)}, u32[]{:S(2)}) async-start(bf16[4,256,1024]{2,1,0:T(8,128)(2,1)} %bitcast.86), calls=%async_computation.3 | async-start | bytes 4194304 | tf_op jit(solution)/shard_map/all_to_all | solution.py:132
  94.5 19.0 %collective-permute-start.4 = (bf16[2,8,128]{2,1,0:T(8,128)(2,1)S(1)}, bf16[2,8,128]{2,1,0:T(8,128)(2,1)S(1)}, u32[]{:S(2)}, u32[]{:S(2)}) collective-permute-start(bf16[2,8,128]{2,1,0:T(8,128)(2,1)S(1)} %convert_element_type.31), channel_id=1, source_target_pairs={{0,256},{128,384},{256,0},{384,128},{1,257},{129,385},{257,1},{385... | collective-permute-start | bytes 12296 | tf_op jit(solution)/shard_map/ppermute | solution.py:136
  102.0 11.6 %collective-permute-start.3 = (bf16[2,8,128]{2,1,0:T(8,128)(2,1)S(1)}, bf16[2,8,128]{2,1,0:T(8,128)(2,1)S(1)}, u32[]{:S(2)}, u32[]{:S(2)}) collective-permute-start(bf16[2,8,128]{2,1,0:T(8,128)(2,1)S(1)} %convert_element_type.31), channel_id=1, source_target_pairs={{0,128},{128,256},{256,384},{384,0},{1,129},{129,257},{257,385},{3... | collective-permute-start | bytes 12296 | tf_op jit(solution)/shard_map/ppermute | solution.py:136
  111.6 9.4 %collective-permute-start.5 = (bf16[2,8,128]{2,1,0:T(8,128)(2,1)S(1)}, bf16[2,8,128]{2,1,0:T(8,128)(2,1)S(1)}, u32[]{:S(2)}, u32[]{:S(2)}) collective-permute-start(bf16[2,8,128]{2,1,0:T(8,128)(2,1)S(1)} %convert_element_type.31), channel_id=1, source_target_pairs={{0,384},{128,0},{256,128},{384,256},{1,385},{129,1},{257,129},{385... | collective-permute-start | bytes 12296 | tf_op jit(solution)/shard_map/ppermute | solution.py:136
  130.0 6.0 %collective-permute-start.6 = (bf16[1024,1024]{1,0:T(8,128)(2,1)S(1)}, bf16[1024,1024]{1,0:T(8,128)(2,1)S(1)}, u32[]{:S(2)}, u32[]{:S(2)}) collective-permute-start(bf16[1024,1024]{1,0:T(8,128)(2,1)S(1)} %bitcast.84), channel_id=1, source_target_pairs={{0,1},{1,0},{2,3},{3,2},{4,5},{5,4},{6,7},{7,6},{8,9},{9,8},{10,11... | collective-permute-start | bytes 6291464 | tf_op jit(solution)/shard_map/ppermute | solution.py:136
  131.9 1.6 copy-start.1
  157.3 18.3 %copy-start.2 = (bf16[32,8,512]{2,1,0:T(8,128)(2,1)S(1)}, bf16[32,8,512]{2,1,0:T(8,128)(2,1)}, u32[]{:S(2)}) copy-start(bf16[32,8,512]{2,1,0:T(8,128)(2,1)} %param.10) | copy-start | bytes 786436
  158.2 17.3 %all-to-all-start.5 = ((bf16[16,12,8,128]{3,2,1,0:T(8,128)(2,1)}), bf16[16,12,8,128]{3,2,1,0:T(8,128)(2,1)S(1)}, u32[]{:S(2)}, u32[]{:S(2)}) async-start(bf16[16,12,8,128]{3,2,1,0:T(8,128)(2,1)} %copy.48), calls=%async_computation.5 | async-start | bytes 786432 | tf_op jit(solution)/shard_map/all_to_all | solution.py:132
Sparse Core Ops, SparseCore 0:
  30.4 95.3 all-gather.2

commit v4 on v2

--- a/solution.py
+++ b/solution.py
@@ -80,7 +80,8 @@
     )(where, bounds, query, far, near)
 
 
-def project_kernel(rows_ref, weight_ref, out_ref):
+def project_kernel(core_ref, rows_ref, weight_ref, out_ref):
+    del core_ref
     for part in range(4):
         rows = slice(part * 256, (part + 1) * 256)
         product = jnp.dot(rows_ref[rows], weight_ref[...], preferred_element_type=jnp.float32)
@@ -88,19 +89,24 @@
             out_ref[y, rows] = product[:, y * 128 : (y + 1) * 128].astype(out_ref.dtype)
 
 
-def project(rows, weight, half, dtype):
-    vmem = pl.BlockSpec(memory_space=pltpu.VMEM)
+def project(core, rows, weight, dtype):
     return pl.pallas_call(
         project_kernel,
-        grid=(1,),
+        grid_spec=pltpu.PrefetchScalarGridSpec(
+            num_scalar_prefetch=1,
+            grid=(1,),
+            in_specs=[
+                pl.BlockSpec(memory_space=pltpu.VMEM),
+                pl.BlockSpec((1024, 512), lambda i, core: (0, core[0])),
+            ],
+            out_specs=pl.BlockSpec(memory_space=pltpu.VMEM),
+        ),
         out_shape=jax.ShapeDtypeStruct((4, 1024, 128), dtype),
-        in_specs=[vmem, pl.BlockSpec((1024, 512), lambda i: (0, half))],
-        out_specs=vmem,
         compiler_params=pltpu.CompilerParams(vmem_limit_bytes=32 * 1024 * 1024),
         cost_estimate=pl.CostEstimate(
             flops=2 * 1024 * 1024 * 512, bytes_accessed=4 * 1024 * 1024, transcendentals=0
         ),
-    )(rows, weight)
+    )(core.astype(jnp.int32).reshape(1), rows, weight)
 
 
 def swap(source, axes, split=0, concat=0):
@@ -118,7 +124,7 @@
     beta = 4 * zl + x
 
     weight = out_weight.reshape(8, 2, 4, 2, 4, 128)
-    weight = jnp.where(core == 0, weight, jnp.flip(weight, 3)).transpose(4, 0, 1, 3, 2, 5).reshape(4, 8, 2, 1024)
+    weight = weight.transpose(4, 0, 1, 3, 2, 5).reshape(4, 8, 2, 1024)
     weight = swap(weight, "x").transpose(1, 0, 2, 3).reshape(8, 8, 1024)
     gathered = lax.all_gather(weight, Z, axis=0, tiled=False)
     gathered = gathered.transpose(1, 0, 2, 3).reshape(1024, 1024)
@@ -159,9 +165,9 @@
 
     wide = swap(attended.reshape(4, 256, 1024), "x").reshape(1024, 1024)
     wide, packed = lax.optimization_barrier((wide, packed))
-    theirs = project(wide, gathered, 1, bf16)
+    theirs = project(1 - core, wide, gathered, bf16)
     got = lax.ppermute(theirs, "c", [(0, 1), (1, 0)])
-    ours = project(wide, gathered, 0, f32)
+    ours = project(core, wide, gathered, f32)
     ours, got = lax.optimization_barrier((ours, got))
     parts = swap((ours + got.astype(f32)).astype(bf16), "y")
     summed = jnp.sum(parts.astype(f32), axis=0).astype(bf16)

time: 176 us -> 176 us (level)
  no operation moved by 1% of the time
where the time goes in v4:
time: 176 us; the launch traced here: 175 us
  starting transfers between devices  68.9 us (39%)
  waiting for transfers between devices  52.9 us (30%)
  blocking collectives  18.8 us (11%)
  between operations  14.5 us (8%)
  Pallas kernels  8.29 us (5%)
  local copies, waits for them, and re-layouts  6.87 us (4%)
  other arithmetic  4.69 us (3%)
    ppermute x6, starting transfers between devices, shift(): lax.ppermute(source, axes, [(i, (i + step) % size) for i in range(size)])  40.5 us
    all_to_all x5, starting transfers between devices, swap(): lax.all_to_all(source, axes, split_axis=split, concat_axis=concat, tiled=...  26.4 us
    all_to_all x5, waiting for transfers between devices, swap(): lax.all_to_all(source, axes, split_axis=split, concat_axis=concat, tiled=...  25 us
    ppermute x6, waiting for transfers between devices, shift(): lax.ppermute(source, axes, [(i, (i + step) % size) for i in range(size)])  23.6 us
    all_to_all x1, blocking collectives, swap(): lax.all_to_all(source, axes, split_axis=split, concat_axis=concat, tiled=...  18.8 us
    pallas_call x1, Pallas kernels, attend(): pl.pallas_call(attend_kernel, out_shape=(jax.ShapeDtypeStruct((4, 2, ROWS...  5.79 us
  transfers between devices with their start and end apart: 13, of which 8 were waited for; matrix products, arithmetic and copies ran while one was open for 2% of the time, Pallas kernels for 4%

profile of v4, /device:TPU:8, one launch (start us, length us, event | category | flops | bytes accessed | tf_op | source)
XLA Modules:
  0.0 174.9 jit_solution(8233716885759069394)
XLA Ops:
  7.2 1.0 reshape.156
  8.3 0.7 reshape.157
  9.0 4.3 %all-to-all-start.3 = ((bf16[4,8,2,1024]{3,1,2,0:T(8,128)(2,1)}), bf16[4,8,2,1024]{3,1,2,0:T(8,128)(2,1)S(1)}, u32[]{:S(2)}, u32[]{:S(2)}) async-start(bf16[4,8,2,1024]{3,1,2,0:T(8,128)(2,1)} %reshape.157), calls=%async_computation.3 | async-start | bytes 262144 | tf_op jit(solution)/shard_map/all_to_all | solution.py:113
  13.3 0.9 pad_maximum_fusion.3
  14.2 0.7 pad_maximum_fusion.2
  14.9 4.4 %all-to-all-done.3 = bf16[4,8,2,1024]{3,1,2,0:T(8,128)(2,1)S(1)} async-done(((bf16[4,8,2,1024]{3,1,2,0:T(8,128)(2,1)}), bf16[4,8,2,1024]{3,1,2,0:T(8,128)(2,1)S(1)}, u32[]{:S(2)}, u32[]{:S(2)}) %all-to-all-start.3) | async-done | bytes 131104 | tf_op jit(solution)/shard_map/all_to_all | solution.py:113
  19.2 6.6 %all-to-all-start = ((bf16[16,3,8,256]{3,2,1,0:T(8,128)(2,1)}), bf16[16,3,8,256]{3,2,1,0:T(8,128)(2,1)S(1)}, u32[]{:S(2)}, u32[]{:S(2)}) async-start(bf16[16,3,8,256]{3,2,1,0:T(8,128)(2,1)} %pad_maximum_fusion.2), calls=%async_computation | async-start | bytes 393216 | tf_op jit(solution)/shard_map/all_to_all | solution.py:113
  25.9 0.7 copy.45
  26.7 8.7 %all-to-all-done = bf16[16,3,8,256]{3,2,1,0:T(8,128)(2,1)S(1)} async-done(((bf16[16,3,8,256]{3,2,1,0:T(8,128)(2,1)}), bf16[16,3,8,256]{3,2,1,0:T(8,128)(2,1)S(1)}, u32[]{:S(2)}, u32[]{:S(2)}) %all-to-all-start) | async-done | bytes 196640 | tf_op jit(solution)/shard_map/all_to_all | solution.py:113
  35.3 3.6 %all-to-all-start.1 = ((bf16[32,8,1024]{2,1,0:T(8,128)(2,1)}), bf16[32,8,1024]{2,1,0:T(8,128)(2,1)S(1)}, u32[]{:S(2)}, u32[]{:S(2)}) async-start(bf16[32,8,1024]{2,1,0:T(8,128)(2,1)} %param.7), calls=%async_computation.1 | async-start | bytes 1048576 | tf_op jit(solution)/shard_map/all_to_all | solution.py:113
  39.0 0.1 add_multiply_fusion.1
  39.1 0.1 iota_add_fusion
  39.2 0.1 fusion.1
  39.2 0.1 add_multiply_fusion
  39.4 9.1 %collective-permute-start = (bf16[2,128,256]{2,1,0:T(8,128)(2,1)S(1)}, bf16[2,128,256]{2,1,0:T(8,128)(2,1)S(1)}, u32[]{:S(2)}, u32[]{:S(2)}) collective-permute-start(bf16[2,128,256]{2,1,0:T(8,128)(2,1)S(1)} %bitcast.106), channel_id=1, source_target_pairs={{0,128},{128,256},{256,384},{384,0},{1,129},{129,257},{257,385},{3... | collective-permute-start | bytes 393224 | tf_op jit(solution)/shard_map/ppermute | solution.py:117
  48.5 2.9 %collective-permute-start.2 = (bf16[2,128,256]{2,1,0:T(8,128)(2,1)S(1)}, bf16[2,128,256]{2,1,0:T(8,128)(2,1)S(1)}, u32[]{:S(2)}, u32[]{:S(2)}) collective-permute-start(bf16[2,128,256]{2,1,0:T(8,128)(2,1)S(1)} %bitcast.105), channel_id=1, source_target_pairs={{0,384},{128,0},{256,128},{384,256},{1,385},{129,1},{257,129},{385... | collective-permute-start | bytes 393224 | tf_op jit(solution)/shard_map/ppermute | solution.py:117
  51.4 10.8 %collective-permute-start.1 = (bf16[2,128,256]{2,1,0:T(8,128)(2,1)S(1)}, bf16[2,128,256]{2,1,0:T(8,128)(2,1)S(1)}, u32[]{:S(2)}, u32[]{:S(2)}) collective-permute-start(bf16[2,128,256]{2,1,0:T(8,128)(2,1)S(1)} %bitcast.104), channel_id=1, source_target_pairs={{0,256},{128,384},{256,0},{384,128},{1,257},{129,385},{257,1},{385... | collective-permute-start | bytes 393224 | tf_op jit(solution)/shard_map/ppermute | solution.py:117
  62.2 0.1 pad_add_fusion.where_ref
  62.3 0.3 convert_reduce_fusion.1
  62.6 10.1 %collective-permute-done = bf16[2,128,256]{2,1,0:T(8,128)(2,1)S(1)} collective-permute-done((bf16[2,128,256]{2,1,0:T(8,128)(2,1)S(1)}, bf16[2,128,256]{2,1,0:T(8,128)(2,1)S(1)}, u32[]{:S(2)}, u32[]{:S(2)}) %collective-permute-start) | collective-permute-done | bytes 131104 | tf_op jit(solution)/shard_map/ppermute | solution.py:117
  72.7 6.1 %collective-permute-done.1 = bf16[2,128,256]{2,1,0:T(8,128)(2,1)S(1)} collective-permute-done((bf16[2,128,256]{2,1,0:T(8,128)(2,1)S(1)}, bf16[2,128,256]{2,1,0:T(8,128)(2,1)S(1)}, u32[]{:S(2)}, u32[]{:S(2)}) %collective-permute-start.1) | collective-permute-done | bytes 131104 | tf_op jit(solution)/shard_map/ppermute | solution.py:117
  78.9 5.8 %shard_map.86 = (bf16[4,2,128,1024]{3,2,1,0:T(8,128)(2,1)S(1)}, f32[2,8,128]{2,1,0:T(8,128)S(1)}) custom-call(s32[2]{0:T(128)S(1)} %pad_add_fusion.where_ref, s32[1,128]{1,0:T(1,128)S(1)} %get-tuple-element.31.bounds_ref, bf16[2,128,1024]{2,1,0:T(8,128)(2,1)S(1)} %bitcast.92, bf16[4,2,128,256]{3,2,1,0:T(8,128)(2,1)S(1)} %pad_maximum_fusion.far_ref, ...), custom_call_target="tpu_custom_call" | custom-call | flops 671088640 | bytes 2097152 | tf_op jit(solution)/shard_map/pallas_call | solution.py:68
  84.7 1.3 copy-done.2
  86.0 6.2 %all-to-all-start.2 = ((bf16[4,256,1024]{2,1,0:T(8,128)(2,1)}), bf16[4,256,1024]{2,1,0:T(8,128)(2,1)S(1)}, u32[]{:S(2)}, u32[]{:S(2)}) async-start(bf16[4,256,1024]{2,1,0:T(8,128)(2,1)} %bitcast.91), calls=%async_computation.2 | async-start | bytes 4194304 | tf_op jit(solution)/shard_map/all_to_all | solution.py:113
  92.2 0.3 select_reduce_fusion
  92.5 0.1 broadcast_in_dim.58
  92.6 0.1 eq.65
  92.7 0.1 broadcast_in_dim.63
  92.7 0.1 eq.69
  92.9 5.3 %collective-permute-start.4 = (bf16[2,8,128]{2,1,0:T(8,128)(2,1)S(1)}, bf16[2,8,128]{2,1,0:T(8,128)(2,1)S(1)}, u32[]{:S(2)}, u32[]{:S(2)}) collective-permute-start(bf16[2,8,128]{2,1,0:T(8,128)(2,1)S(1)} %convert_element_type.37), channel_id=1, source_target_pairs={{0,256},{128,384},{256,0},{384,128},{1,257},{129,385},{257,1},{385... | collective-permute-start | bytes 12296 | tf_op jit(solution)/shard_map/ppermute | solution.py:117
  98.1 10.5 %collective-permute-start.3 = (bf16[2,8,128]{2,1,0:T(8,128)(2,1)S(1)}, bf16[2,8,128]{2,1,0:T(8,128)(2,1)S(1)}, u32[]{:S(2)}, u32[]{:S(2)}) collective-permute-start(bf16[2,8,128]{2,1,0:T(8,128)(2,1)S(1)} %convert_element_type.37), channel_id=1, source_target_pairs={{0,128},{128,256},{256,384},{384,0},{1,129},{129,257},{257,385},{3... | collective-permute-start | bytes 12296 | tf_op jit(solution)/shard_map/ppermute | solution.py:117
  108.7 1.9 %collective-permute-start.5 = (bf16[2,8,128]{2,1,0:T(8,128)(2,1)S(1)}, bf16[2,8,128]{2,1,0:T(8,128)(2,1)S(1)}, u32[]{:S(2)}, u32[]{:S(2)}) collective-permute-start(bf16[2,8,128]{2,1,0:T(8,128)(2,1)S(1)} %convert_element_type.37), channel_id=1, source_target_pairs={{0,384},{128,0},{256,128},{384,256},{1,385},{129,1},{257,129},{385... | collective-permute-start | bytes 12296 | tf_op jit(solution)/shard_map/ppermute | solution.py:117
  110.6 7.4 %collective-permute-done.5 = bf16[2,8,128]{2,1,0:T(8,128)(2,1)S(1)} collective-permute-done((bf16[2,8,128]{2,1,0:T(8,128)(2,1)S(1)}, bf16[2,8,128]{2,1,0:T(8,128)(2,1)S(1)}, u32[]{:S(2)}, u32[]{:S(2)}) %collective-permute-start.5) | collective-permute-done | bytes 4128 | tf_op jit(solution)/shard_map/ppermute | solution.py:117
  118.1 0.1 select_add_fusion
  118.2 2.9 %all-gather.2.cloned.1.call-done = bf16[16,8,8,1024]{3,2,0,1:T(8,128)(2,1)} async-done(((bf16[1,8,8,1024]{3,2,0,1:T(8,128)(2,1)}), bf16[16,8,8,1024]{3,2,0,1:T(8,128)(2,1)}) %all-gather.2.cloned.1.call-update) | async-done | bytes 2097168 | tf_op jit(solution)/shard_map/all_gather | solution.py:129
  121.1 1.6 copy-done
  122.7 1.2 shard_map.88
  123.9 1.9 %collective-permute-start.6 = (bf16[4,1024,128]{2,1,0:T(8,128)(2,1)S(1)}, bf16[4,1024,128]{2,1,0:T(8,128)(2,1)S(1)}, u32[]{:S(2)}, u32[]{:S(2)}) collective-permute-start(bf16[4,1024,128]{2,1,0:T(8,128)(2,1)S(1)} %shard_map.88), channel_id=1, source_target_pairs={{0,1},{1,0},{2,3},{3,2},{4,5},{5,4},{6,7},{7,6},{8,9},{9,8},{10,11... | collective-permute-start | bytes 3145736 | tf_op jit(solution)/shard_map/ppermute | solution.py:169
  125.9 1.2 shard_map.87
  127.1 1.4 collective-permute-done.6
  128.5 0.2 add_convert_fusion
  128.8 18.8 %all_to_all.43 = bf16[4,1024,128]{2,1,0:T(8,128)(2,1)S(1)} all-to-all(bf16[4,1024,128]{2,1,0:T(8,128)(2,1)S(1)} %add_convert_fusion), channel_id=1, replica_groups=mesh['za'=2,'zb'=2,'zl'=4,'x'=4,'y'=4,'c'=2] {'y'}, dimensions={0} | all-to-all | bytes 2097152 | tf_op jit(solution)/shard_map/all_to_all | solution.py:113
  147.6 0.3 reduce_sum.41
  147.9 0.8 copy.46
  148.7 5.8 %all-to-all-start.5 = ((bf16[16,12,8,128]{3,2,1,0:T(8,128)(2,1)}), bf16[16,12,8,128]{3,2,1,0:T(8,128)(2,1)S(1)}, u32[]{:S(2)}, u32[]{:S(2)}) async-start(bf16[16,12,8,128]{3,2,1,0:T(8,128)(2,1)} %copy.46), calls=%async_computation.5 | async-start | bytes 786432 | tf_op jit(solution)/shard_map/all_to_all | solution.py:113
  154.5 12.0 %all-to-all-done.5 = bf16[16,12,8,128]{3,2,1,0:T(8,128)(2,1)S(1)} async-done(((bf16[16,12,8,128]{3,2,1,0:T(8,128)(2,1)}), bf16[16,12,8,128]{3,2,1,0:T(8,128)(2,1)S(1)}, u32[]{:S(2)}, u32[]{:S(2)}) %all-to-all-start.5) | async-done | bytes 393248 | tf_op jit(solution)/shard_map/all_to_all | solution.py:113
  166.6 0.8 add_convert_fusion.1
  167.5 0.6 maximum_bitcast_fusion
  (43 shorter events, 0.6 us)
Async XLA Ops:
  7.2 32.0 %copy-start.4 = (s32[129]{0:T(256)S(1)}, s32[129]{0:T(256)}, u32[]{:S(2)}) copy-start(s32[129]{0:T(256)} %param.12) | copy-start | bytes 1552
  9.0 10.3 %all-to-all-start.3 = ((bf16[4,8,2,1024]{3,1,2,0:T(8,128)(2,1)}), bf16[4,8,2,1024]{3,1,2,0:T(8,128)(2,1)S(1)}, u32[]{:S(2)}, u32[]{:S(2)}) async-start(bf16[4,8,2,1024]{3,1,2,0:T(8,128)(2,1)} %reshape.157), calls=%async_computation.3 | async-start | bytes 262144 | tf_op jit(solution)/shard_map/all_to_all | solution.py:113
  19.2 16.1 %all-to-all-start = ((bf16[16,3,8,256]{3,2,1,0:T(8,128)(2,1)}), bf16[16,3,8,256]{3,2,1,0:T(8,128)(2,1)S(1)}, u32[]{:S(2)}, u32[]{:S(2)}) async-start(bf16[16,3,8,256]{3,2,1,0:T(8,128)(2,1)} %pad_maximum_fusion.2), calls=%async_computation | async-start | bytes 393216 | tf_op jit(solution)/shard_map/all_to_all | solution.py:113
  25.9 95.2 %all-gather.2.cloned.1.call-start = ((), (), s32[]{:S(2)}) async-start(), calls=%async_computation.6 | async-start | bytes 2228224 | tf_op jit(solution)/shard_map/all_gather | solution.py:129
  35.3 43.5 %all-to-all-start.1 = ((bf16[32,8,1024]{2,1,0:T(8,128)(2,1)}), bf16[32,8,1024]{2,1,0:T(8,128)(2,1)S(1)}, u32[]{:S(2)}, u32[]{:S(2)}) async-start(bf16[32,8,1024]{2,1,0:T(8,128)(2,1)} %param.7), calls=%async_computation.1 | async-start | bytes 1048576 | tf_op jit(solution)/shard_map/all_to_all | solution.py:113
  39.4 33.3 %collective-permute-start = (bf16[2,128,256]{2,1,0:T(8,128)(2,1)S(1)}, bf16[2,128,256]{2,1,0:T(8,128)(2,1)S(1)}, u32[]{:S(2)}, u32[]{:S(2)}) collective-permute-start(bf16[2,128,256]{2,1,0:T(8,128)(2,1)S(1)} %bitcast.106), channel_id=1, source_target_pairs={{0,128},{128,256},{256,384},{384,0},{1,129},{129,257},{257,385},{3... | collective-permute-start | bytes 393224 | tf_op jit(solution)/shard_map/ppermute | solution.py:117
  48.5 24.2 %collective-permute-start.2 = (bf16[2,128,256]{2,1,0:T(8,128)(2,1)S(1)}, bf16[2,128,256]{2,1,0:T(8,128)(2,1)S(1)}, u32[]{:S(2)}, u32[]{:S(2)}) collective-permute-start(bf16[2,128,256]{2,1,0:T(8,128)(2,1)S(1)} %bitcast.105), channel_id=1, source_target_pairs={{0,384},{128,0},{256,128},{384,256},{1,385},{129,1},{257,129},{385... | collective-permute-start | bytes 393224 | tf_op jit(solution)/shard_map/ppermute | solution.py:117
  51.4 27.4 %collective-permute-start.1 = (bf16[2,128,256]{2,1,0:T(8,128)(2,1)S(1)}, bf16[2,128,256]{2,1,0:T(8,128)(2,1)S(1)}, u32[]{:S(2)}, u32[]{:S(2)}) collective-permute-start(bf16[2,128,256]{2,1,0:T(8,128)(2,1)S(1)} %bitcast.104), channel_id=1, source_target_pairs={{0,256},{128,384},{256,0},{384,128},{1,257},{129,385},{257,1},{385... | collective-permute-start | bytes 393224 | tf_op jit(solution)/shard_map/ppermute | solution.py:117
  84.7 1.3 copy-start.2
  86.0 6.2 %copy-start.5 = (s32[128]{0:T(128)S(1)}, s32[128]{0:T(128)}, u32[]{:S(2)}) copy-start(s32[128]{0:T(128)} %param.13) | copy-start | bytes 1540
  86.0 32.2 %all-to-all-start.2 = ((bf16[4,256,1024]{2,1,0:T(8,128)(2,1)}), bf16[4,256,1024]{2,1,0:T(8,128)(2,1)S(1)}, u32[]{:S(2)}, u32[]{:S(2)}) async-start(bf16[4,256,1024]{2,1,0:T(8,128)(2,1)} %bitcast.91), calls=%async_computation.2 | async-start | bytes 4194304 | tf_op jit(solution)/shard_map/all_to_all | solution.py:113
  92.9 17.7 %collective-permute-start.4 = (bf16[2,8,128]{2,1,0:T(8,128)(2,1)S(1)}, bf16[2,8,128]{2,1,0:T(8,128)(2,1)S(1)}, u32[]{:S(2)}, u32[]{:S(2)}) collective-permute-start(bf16[2,8,128]{2,1,0:T(8,128)(2,1)S(1)} %convert_element_type.37), channel_id=1, source_target_pairs={{0,256},{128,384},{256,0},{384,128},{1,257},{129,385},{257,1},{385... | collective-permute-start | bytes 12296 | tf_op jit(solution)/shard_map/ppermute | solution.py:117
  98.1 12.5 %collective-permute-start.3 = (bf16[2,8,128]{2,1,0:T(8,128)(2,1)S(1)}, bf16[2,8,128]{2,1,0:T(8,128)(2,1)S(1)}, u32[]{:S(2)}, u32[]{:S(2)}) collective-permute-start(bf16[2,8,128]{2,1,0:T(8,128)(2,1)S(1)} %convert_element_type.37), channel_id=1, source_target_pairs={{0,128},{128,256},{256,384},{384,0},{1,129},{129,257},{257,385},{3... | collective-permute-start | bytes 12296 | tf_op jit(solution)/shard_map/ppermute | solution.py:117
  108.7 9.4 %collective-permute-start.5 = (bf16[2,8,128]{2,1,0:T(8,128)(2,1)S(1)}, bf16[2,8,128]{2,1,0:T(8,128)(2,1)S(1)}, u32[]{:S(2)}, u32[]{:S(2)}) collective-permute-start(bf16[2,8,128]{2,1,0:T(8,128)(2,1)S(1)} %convert_element_type.37), channel_id=1, source_target_pairs={{0,384},{128,0},{256,128},{384,256},{1,385},{129,1},{257,129},{385... | collective-permute-start | bytes 12296 | tf_op jit(solution)/shard_map/ppermute | solution.py:117
  121.1 1.6 copy-start
  122.7 3.2 %copy-start.1 = (bf16[16,8,8,1024]{3,2,0,1:T(8,128)(2,1)S(1)}, bf16[16,8,8,1024]{3,2,0,1:T(8,128)(2,1)}, u32[]{:S(2)}) copy-start(bf16[16,8,8,1024]{3,2,0,1:T(8,128)(2,1)} %all-gather.2.cloned.1.call-done) | copy-start | bytes 6291460
  123.9 4.6 %collective-permute-start.6 = (bf16[4,1024,128]{2,1,0:T(8,128)(2,1)S(1)}, bf16[4,1024,128]{2,1,0:T(8,128)(2,1)S(1)}, u32[]{:S(2)}, u32[]{:S(2)}) collective-permute-start(bf16[4,1024,128]{2,1,0:T(8,128)(2,1)S(1)} %shard_map.88), channel_id=1, source_target_pairs={{0,1},{1,0},{2,3},{3,2},{4,5},{5,4},{6,7},{7,6},{8,9},{9,8},{10,11... | collective-permute-start | bytes 3145736 | tf_op jit(solution)/shard_map/ppermute | solution.py:169
  147.9 18.7 %copy-start.3 = (bf16[32,8,512]{2,1,0:T(8,128)(2,1)S(1)}, bf16[32,8,512]{2,1,0:T(8,128)(2,1)}, u32[]{:S(2)}) copy-start(bf16[32,8,512]{2,1,0:T(8,128)(2,1)} %param.10) | copy-start | bytes 786436
  148.7 17.8 %all-to-all-start.5 = ((bf16[16,12,8,128]{3,2,1,0:T(8,128)(2,1)}), bf16[16,12,8,128]{3,2,1,0:T(8,128)(2,1)S(1)}, u32[]{:S(2)}, u32[]{:S(2)}) async-start(bf16[16,12,8,128]{3,2,1,0:T(8,128)(2,1)} %copy.46), calls=%async_computation.5 | async-start | bytes 786432 | tf_op jit(solution)/shard_map/all_to_all | solution.py:113
Sparse Core Ops, SparseCore 0:
  28.8 92.2 all-gather.1
